TPU v7x, 32 devices: a whole 2x2x4 slice. The times are simulated.
32 devices in a mesh: seq: 8 (over z, x), tensor: 4 (over y, core).
Axes of the slice: x: 2, y: 2, z: 4, core: 2. Of those that a mesh axis runs over, the one named last changes fastest.
Arguments:
- inputs: bfloat16 [2, 4096, 1024], P(None, 'seq'), may hold values from -6 to 6
- out_grad: bfloat16 [2, 4096, 1024], P(None, 'seq'), may hold values from -6 to 6
- lengths: int32 [2], replicated, may hold values from 2048 to 4096, as said below
- norm_gain: float32 [1024], replicated, may hold values from 0.5 to 1.5
- query_weight: bfloat16 [1024, 1024], P(None, 'tensor'), may hold values from -0.1875 to 0.1875
- key_weight: bfloat16 [1024, 1024], P(None, 'tensor'), may hold values from -0.1875 to 0.1875
- value_weight: bfloat16 [1024, 1024], P(None, 'tensor'), may hold values from -0.1875 to 0.1875
- out_weight: bfloat16 [1024, 1024], P('tensor'), may hold values from -1.5 to 1.5
- mlp_gain: float32 [1024], replicated, may hold values from 0.5 to 1.5
- up_weight: bfloat16 [1024, 4096], P(None, 'tensor'), may hold values from -0.1875 to 0.1875
- down_weight: bfloat16 [4096, 1024], P('tensor'), may hold values from -0.09375 to 0.09375
- decay_rate: float32 [16, 1024], P(None, 'tensor'), may hold values from 0.00012207031 to 0.03
- state_input: float32 [16, 1024], P(None, 'tensor'), may hold values from -4 to 4
- state_output: float32 [16, 1024], P(None, 'tensor'), may hold values from -1.5 to 1.5
- skip_gain: float32 [1024], P('tensor'), may hold values from -4 to 4
Outputs:
- outputs: bfloat16 [2, 4096, 1024], P(None, 'seq')
- input_grad: bfloat16 [2, 4096, 1024], P(None, 'seq', 'tensor')
- norm_gain_grad: float32 [1024], P('tensor')
- query_weight_grad: float32 [1024, 1024], P(None, 'tensor')
- key_weight_grad: float32 [1024, 1024], P(None, 'tensor')
- value_weight_grad: float32 [1024, 1024], P(None, 'tensor')
- out_weight_grad: float32 [1024, 1024], P('tensor')
- mlp_gain_grad: float32 [1024], replicated
- up_weight_grad: float32 [1024, 4096], P(None, 'tensor')
- down_weight_grad: float32 [4096, 1024], P('tensor')
- decay_rate_grad: float32 [16, 1024], P(None, 'tensor')
- state_input_grad: float32 [16, 1024], P(None, 'tensor')
- state_output_grad: float32 [16, 1024], P(None, 'tensor')
- skip_gain_grad: float32 [1024], P('tensor')
Inputs may be any that keep to these rules, and one draw needn't show every extreme that they name: `lengths`: one sequence has length 4096 in every draw.
All inputs are finite; a program needn't handle non-finite values.
Results may differ from a plain program's by a relative error of at most 0.02.
Values may be sent and summed in bfloat16 or wider, within the bound.
No kernel may reach another device: no remote copies, remote signals or barrier semaphores. Data moves between devices by JAX's collectives and lax.ppermute only.
A program may use at most 320 MiB of HBM per device.

v0:
```python
import math

import jax
import jax.numpy as jnp
from jax import lax
from jax.sharding import PartitionSpec as P

HD = 128
NS = 16
CTX = 128


epsilon = 1e-06
highest = lax.Precision.HIGHEST


def entering_2(value, axis, join, neutral):
    count, mine = (lax.axis_size(axis), lax.axis_index(axis))
    pieces = jax.tree.map(lambda part: lax.all_gather(part, axis), value)
    so_far = jax.tree.map(
        lambda part, zero: jnp.full_like(part, 0) + jnp.asarray(zero, part.dtype), value, neutral
    )

    def turn(position, so_far):
        longer = join(so_far, jax.tree.map(lambda part: part[position], pieces))
        return jax.tree.map(lambda new, old: jnp.where(position < mine, new, old), longer, so_far)

    return lax.fori_loop(0, count - 1, turn, so_far)


def carried_in(value, axis, join, neutral):
    count = lax.axis_size(axis)
    place = lax.axis_index(axis)
    ahead = count - 1 - place
    gathered = jax.tree.map(
        lambda a, kind: lax.all_gather(a.astype(kind), axis), value, (jnp.bfloat16, jnp.bfloat16)
    )
    state = jax.tree.map(lambda a, e: jnp.zeros_like(a) + jnp.asarray(e, a.dtype), value, neutral)

    def one(turn, state):
        source = count - 1 - turn
        return join(
            state,
            jax.tree.map(
                lambda a, own: lax.dynamic_index_in_dim(a, source, 0, False).astype(own.dtype),
                gathered,
                value,
            ),
        )

    return lax.fori_loop(0, ahead, one, state)


def combine_pair(early, late):
    return (early[0] * late[0], late[0] * early[1] + late[1])


def exact_gelu(value):
    return jax.nn.gelu(value, approximate=False)


def state_params(rate, weight_in):
    return (jnp.exp(-rate), jnp.sqrt(-jnp.expm1(-2.0 * rate)) * weight_in)


def power_table(rate, lag):
    steps = jnp.maximum(lag, 0).astype(jnp.float32)
    return jnp.where(
        (lag >= 0)[:, :, None, None], jnp.exp(-rate[None, None] * steps[:, :, None, None]), 0.0
    )


def run_states(rate, sources, later):
    count = sources.shape[0]
    span = math.gcd(count, 32)
    groups = count // span
    pieces = sources.reshape(groups, span, sources.shape[1], sources.shape[2])
    inner_ids = jnp.arange(span)
    group_ids = jnp.arange(groups)
    if later:
        inner_lag = inner_ids[None, :] - inner_ids[:, None]
        group_lag = group_ids[None, :] - group_ids[:, None] - 1
    else:
        inner_lag = inner_ids[:, None] - inner_ids[None, :]
        group_lag = group_ids[:, None] - group_ids[None, :] - 1
    inner = jnp.einsum("tsnc,gsnc->gtnc", power_table(rate, inner_lag), pieces, precision=highest)
    if later:
        edges = inner[:, 0]
        reach = (span - inner_ids).astype(jnp.float32)
    else:
        edges = inner[:, -1]
        reach = (inner_ids + 1).astype(jnp.float32)
    group_pow = jnp.where(
        (group_lag >= 0)[:, :, None, None],
        jnp.exp(
            -rate[None, None]
            * (span * jnp.maximum(group_lag, 0)).astype(jnp.float32)[:, :, None, None]
        ),
        0.0,
    )
    entering = jnp.einsum("gjnc,jnc->gnc", group_pow, edges, precision=highest)
    reach_pow = jnp.exp(-rate[None] * reach[:, None, None])
    full = inner + reach_pow[None] * entering[:, None]
    return full.reshape(sources.shape)


def local(
    inputs,
    out_grad,
    lengths,
    norm_gain,
    query_weight,
    key_weight,
    value_weight,
    out_weight,
    mlp_gain,
    up_weight,
    down_weight,
    decay_rate,
    state_input,
    state_output,
    skip_gain,
):
    seqs, block, width = inputs.shape
    local_width = query_weight.shape[1]
    heads_here = local_width // HD
    stride = block // CTX
    scale = HD ** (-0.5)
    tensor_index = lax.axis_index("tensor")
    seq_index = lax.axis_index("seq")
    tensor_count = lax.axis_size("tensor")
    channel_start = tensor_index * local_width
    rows_here = block // tensor_count
    row_start = tensor_index * rows_here
    positions = seq_index * block + jnp.arange(block)
    valid = (positions[None, :] < lengths[:, None]).astype(jnp.float32)
    full_in = inputs.astype(jnp.float32)
    inverse1 = lax.rsqrt(jnp.mean(full_in * full_in, -1, keepdims=True) + epsilon)
    hat_one = full_in * inverse1
    normed1 = hat_one * norm_gain
    normed_low = normed1.astype(jnp.bfloat16)
    chan_in = lax.dynamic_slice_in_dim(normed1, channel_start, local_width, 2)
    decay, in_coeff = state_params(decay_rate, state_input)
    step_count = jnp.arange(block).astype(jnp.float32)
    powers = jnp.exp(-decay_rate[None] * (step_count + 1.0)[:, None, None])
    back_powers = jnp.exp(-decay_rate[None] * (block - 1.0 - step_count)[:, None, None])

    def local_states(chan_seq):
        return run_states(decay_rate, in_coeff[None] * chan_seq[:, None, :], False)

    state_local = lax.map(local_states, chan_in)
    finals = state_local[:, -1]
    block_decay = jnp.broadcast_to(jnp.exp(-decay_rate * block), finals.shape)
    identity = (jnp.ones_like(finals), jnp.zeros_like(finals))
    carry_in = entering_2((block_decay, finals), "seq", combine_pair, identity)[1]
    ctx_local = state_local.reshape(seqs, CTX, stride, NS, local_width)[:, :, stride - 1]
    ctx_powers = powers.reshape(CTX, stride, NS, local_width)[:, stride - 1]
    ctx_states = ctx_local + ctx_powers[None] * carry_in[:, None]
    ctx_chan = chan_in.reshape(seqs, CTX, stride, local_width)[:, :, stride - 1]
    ctx_out = jnp.sum(state_output[None, None] * ctx_states, 2) + skip_gain * ctx_chan
    ctx_full = lax.all_gather(ctx_out.astype(jnp.bfloat16), "tensor", axis=2, tiled=True)
    query = jnp.dot(normed_low, query_weight, preferred_element_type=jnp.float32).astype(
        jnp.bfloat16
    )
    key_self = jnp.dot(normed_low, key_weight, preferred_element_type=jnp.float32).astype(
        jnp.bfloat16
    )
    value_self = jnp.dot(normed_low, value_weight, preferred_element_type=jnp.float32).astype(
        jnp.bfloat16
    )
    key_ctx = jnp.dot(ctx_full, key_weight, preferred_element_type=jnp.float32).astype(jnp.bfloat16)
    value_ctx = jnp.dot(ctx_full, value_weight, preferred_element_type=jnp.float32).astype(
        jnp.bfloat16
    )
    row_ids = jnp.arange(block)[:, None]
    ctx_cols = stride * jnp.arange(CTX) + stride - 1
    allowed = jnp.concatenate(
        [ctx_cols[None, :] <= row_ids, jnp.arange(block)[None, :] <= row_ids], 1
    )

    def split_heads(value):
        return value.reshape(value.shape[0], heads_here, HD)

    def scores_of(query_seq, keys):
        raw = (
            jnp.einsum(
                "qhd,khd->hqk",
                split_heads(query_seq),
                split_heads(keys),
                preferred_element_type=jnp.float32,
            )
            * scale
        )
        return jnp.where(allowed[None], raw, -1e30)

    def attend_forward(item):
        query_seq, key_own, value_own, key_side, value_side = item
        keys = jnp.concatenate([key_side, key_own], 0)
        values = jnp.concatenate([value_side, value_own], 0)
        scores = scores_of(query_seq, keys)
        top = jnp.max(scores, -1, keepdims=True)
        expo = jnp.exp(scores - top)
        total = jnp.sum(expo, -1, keepdims=True)
        probs_low = (expo / total).astype(jnp.bfloat16)
        result = jnp.einsum(
            "hqk,khd->qhd", probs_low, split_heads(values), preferred_element_type=jnp.float32
        )
        return (result.reshape(block, local_width).astype(jnp.bfloat16), top + jnp.log(total))

    attn_low, log_total = lax.map(attend_forward, (query, key_self, value_self, key_ctx, value_ctx))
    attn_part = jnp.dot(attn_low, out_weight, preferred_element_type=jnp.float32)
    middle = full_in + lax.psum(attn_part.astype(jnp.bfloat16), "tensor").astype(jnp.float32)
    inverse2 = lax.rsqrt(jnp.mean(middle * middle, -1, keepdims=True) + epsilon)
    hat_two = middle * inverse2
    normed2_low = (hat_two * mlp_gain).astype(jnp.bfloat16)
    mid_share = lax.dynamic_slice_in_dim(middle, row_start, rows_here, 1)
    pre_act = jnp.dot(normed2_low, up_weight, preferred_element_type=jnp.float32)
    act_low = exact_gelu(pre_act).astype(jnp.bfloat16)
    mlp_part = jnp.dot(act_low, down_weight, preferred_element_type=jnp.float32)
    mlp_share = lax.psum_scatter(
        mlp_part.astype(jnp.bfloat16), "tensor", scatter_dimension=1, tiled=True
    ).astype(jnp.float32)
    outputs = lax.all_gather(
        (mid_share + mlp_share).astype(jnp.bfloat16), "tensor", axis=1, tiled=True
    )
    cotangent = out_grad.astype(jnp.float32) * valid[:, :, None]
    cot_low = cotangent.astype(jnp.bfloat16)
    down_grad = jnp.einsum("sbf,sbd->fd", act_low, cot_low, preferred_element_type=jnp.float32)
    act_grad = jnp.einsum("sbd,fd->sbf", cot_low, down_weight, preferred_element_type=jnp.float32)
    gelu_pull = jax.vjp(exact_gelu, pre_act)[1]
    pre_grad_low = gelu_pull(act_grad)[0].astype(jnp.bfloat16)
    up_grad = jnp.einsum(
        "sbd,sbf->df", normed2_low, pre_grad_low, preferred_element_type=jnp.float32
    )
    n2_part = jnp.einsum("sbf,df->sbd", pre_grad_low, up_weight, preferred_element_type=jnp.float32)
    n2_grad = lax.psum(n2_part.astype(jnp.bfloat16), "tensor").astype(jnp.float32)
    hat2_grad = n2_grad * mlp_gain
    mid_grad = cotangent + inverse2 * (
        hat2_grad - hat_two * jnp.mean(hat2_grad * hat_two, -1, keepdims=True)
    )
    gain_rows = lax.dynamic_slice_in_dim(n2_grad * hat_two, row_start, rows_here, 1)
    gain_part = jnp.sum(gain_rows, (0, 1))
    mid_low = mid_grad.astype(jnp.bfloat16)
    mid_slice = lax.dynamic_slice_in_dim(mid_grad, channel_start, local_width, 2)
    out_weight_grad = jnp.einsum(
        "sbh,sbd->hd", attn_low, mid_low, preferred_element_type=jnp.float32
    )
    attn_grad_low = jnp.einsum(
        "sbd,hd->sbh", mid_low, out_weight, preferred_element_type=jnp.float32
    ).astype(jnp.bfloat16)

    def attend_back(item):
        query_seq, key_own, value_own, key_side, value_side, grad_low, log_sum = item
        keys = jnp.concatenate([key_side, key_own], 0)
        values = jnp.concatenate([value_side, value_own], 0)
        probs = jnp.exp(scores_of(query_seq, keys) - log_sum)
        grad_heads = split_heads(grad_low)
        prob_grad = jnp.einsum(
            "qhd,khd->hqk", grad_heads, split_heads(values), preferred_element_type=jnp.float32
        )
        row_term = jnp.sum(probs * prob_grad, -1, keepdims=True)
        score_low = (probs * (prob_grad - row_term)).astype(jnp.bfloat16)
        query_back = jnp.einsum(
            "hqk,khd->qhd", score_low, split_heads(keys), preferred_element_type=jnp.float32
        )
        key_back = jnp.einsum(
            "hqk,qhd->khd", score_low, split_heads(query_seq), preferred_element_type=jnp.float32
        )
        value_back = jnp.einsum(
            "hqk,qhd->khd",
            probs.astype(jnp.bfloat16),
            grad_heads,
            preferred_element_type=jnp.float32,
        )
        query_back = (query_back * scale).reshape(block, local_width).astype(jnp.bfloat16)
        key_back = (key_back * scale).reshape(CTX + block, local_width).astype(jnp.bfloat16)
        value_back = value_back.reshape(CTX + block, local_width).astype(jnp.bfloat16)
        return (query_back, key_back[CTX:], value_back[CTX:], key_back[:CTX], value_back[:CTX])

    query_grad, key_own_grad, value_own_grad, key_side_grad, value_side_grad = lax.map(
        attend_back, (query, key_self, value_self, key_ctx, value_ctx, attn_grad_low, log_total)
    )
    query_weight_grad = jnp.einsum(
        "sbd,sbh->dh", normed_low, query_grad, preferred_element_type=jnp.float32
    )
    key_weight_grad = jnp.einsum(
        "sbd,sbh->dh", normed_low, key_own_grad, preferred_element_type=jnp.float32
    ) + jnp.einsum("scd,sch->dh", ctx_full, key_side_grad, preferred_element_type=jnp.float32)
    value_weight_grad = jnp.einsum(
        "sbd,sbh->dh", normed_low, value_own_grad, preferred_element_type=jnp.float32
    ) + jnp.einsum("scd,sch->dh", ctx_full, value_side_grad, preferred_element_type=jnp.float32)
    n1_part = (
        jnp.einsum("sbh,dh->sbd", query_grad, query_weight, preferred_element_type=jnp.float32)
        + jnp.einsum("sbh,dh->sbd", key_own_grad, key_weight, preferred_element_type=jnp.float32)
        + jnp.einsum(
            "sbh,dh->sbd", value_own_grad, value_weight, preferred_element_type=jnp.float32
        )
    )
    ctx_part = jnp.einsum(
        "sch,dh->scd", key_side_grad, key_weight, preferred_element_type=jnp.float32
    ) + jnp.einsum("sch,dh->scd", value_side_grad, value_weight, preferred_element_type=jnp.float32)
    ctx_grad = lax.psum_scatter(
        ctx_part.astype(jnp.bfloat16), "tensor", scatter_dimension=2, tiled=True
    ).astype(jnp.float32)
    zero_rows = jnp.zeros((seqs, CTX, stride - 1, local_width), jnp.float32)
    mixed_grad = jnp.concatenate([zero_rows, ctx_grad[:, :, None]], 2).reshape(
        seqs, block, local_width
    )

    def local_adjoint(grad_seq):
        return run_states(decay_rate, state_output[None] * grad_seq[:, None, :], True)

    adjoint_local = lax.map(local_adjoint, mixed_grad)
    leading = decay[None] * adjoint_local[:, 0]
    carry_back = carried_in((block_decay, leading), "seq", combine_pair, identity)[1]
    state_grad = adjoint_local + back_powers[None] * carry_back[:, None]
    states = state_local + powers[None] * carry_in[:, None]
    previous = jnp.concatenate([carry_in[:, None], states[:, :-1]], 1)
    decay_grad = jnp.sum(state_grad * previous, (0, 1))
    coeff_grad = jnp.sum(state_grad * chan_in[:, :, None, :], (0, 1))
    state_output_grad = jnp.sum(mixed_grad[:, :, None, :] * states, (0, 1))
    skip_gain_grad = jnp.sum(mixed_grad * chan_in, (0, 1))
    chan_grad = skip_gain * mixed_grad + jnp.sum(in_coeff[None, None] * state_grad, 2)
    param_pull = jax.vjp(state_params, decay_rate, state_input)[1]
    decay_rate_grad, state_input_grad = param_pull((decay_grad, coeff_grad))
    n1_share = (
        lax.psum_scatter(
            n1_part.astype(jnp.bfloat16), "tensor", scatter_dimension=2, tiled=True
        ).astype(jnp.float32)
        + chan_grad
    )
    hat_slice = lax.dynamic_slice_in_dim(hat_one, channel_start, local_width, 2)
    gain_slice = lax.dynamic_slice_in_dim(norm_gain, channel_start, local_width, 0)
    norm_gain_grad = jnp.sum(n1_share * hat_slice, (0, 1))
    hat1_grad = n1_share * gain_slice
    mlp_gain_grad, row_total = lax.psum((gain_part, jnp.sum(hat1_grad * hat_slice, -1)), "tensor")
    input_grad = (
        mid_slice + inverse1 * (hat1_grad - hat_slice * (row_total / width)[:, :, None])
    ).astype(jnp.bfloat16)
    summed = (
        lax.psum(norm_gain_grad.astype(jnp.bfloat16), "seq").astype(jnp.float32),
        lax.psum(query_weight_grad.astype(jnp.bfloat16), "seq").astype(jnp.float32),
        lax.psum(key_weight_grad.astype(jnp.bfloat16), "seq").astype(jnp.float32),
        lax.psum(value_weight_grad.astype(jnp.bfloat16), "seq").astype(jnp.float32),
        lax.psum(out_weight_grad.astype(jnp.bfloat16), "seq").astype(jnp.float32),
        lax.psum(mlp_gain_grad.astype(jnp.bfloat16), "seq").astype(jnp.float32),
        lax.psum(up_grad.astype(jnp.bfloat16), "seq").astype(jnp.float32),
        lax.psum(down_grad.astype(jnp.bfloat16), "seq").astype(jnp.float32),
        lax.psum(decay_rate_grad.astype(jnp.bfloat16), "seq").astype(jnp.float32),
        lax.psum(state_input_grad.astype(jnp.bfloat16), "seq").astype(jnp.float32),
        lax.psum(state_output_grad.astype(jnp.bfloat16), "seq").astype(jnp.float32),
        lax.psum(skip_gain_grad.astype(jnp.bfloat16), "seq").astype(jnp.float32),
    )
    return (
        outputs,
        input_grad,
        summed[0],
        summed[1],
        summed[2],
        summed[3],
        summed[4],
        summed[5],
        summed[6],
        summed[7],
        summed[8],
        summed[9],
        summed[10],
        summed[11],
    )


def solution(mesh):
    in_specs = (
        P(None, "seq", None),
        P(None, "seq", None),
        P(),
        P(),
        P(None, "tensor"),
        P(None, "tensor"),
        P(None, "tensor"),
        P("tensor", None),
        P(),
        P(None, "tensor"),
        P("tensor", None),
        P(None, "tensor"),
        P(None, "tensor"),
        P(None, "tensor"),
        P("tensor"),
    )
    out_specs = (
        P(None, "seq", None),
        P(None, "seq", "tensor"),
        P("tensor"),
        P(None, "tensor"),
        P(None, "tensor"),
        P(None, "tensor"),
        P("tensor", None),
        P(),
        P(None, "tensor"),
        P("tensor", None),
        P(None, "tensor"),
        P(None, "tensor"),
        P(None, "tensor"),
        P("tensor"),
    )
    return jax.shard_map(local, mesh=mesh, in_specs=in_specs, out_specs=out_specs, check_vma=False)
```

profile of v0, /device:TPU:0, one launch (start us, length us, event | category | flops | bytes accessed | tf_op | source)
XLA Modules:
  0.0 1338.2 jit_solution(15545494332042853496)
XLA Ops:
  11.8 5.6 convert_multiply_fusion.1
  22.1 8.0 broadcast.478.clone
  30.1 423.2 %while.82 = (s32[]{:T(128)}, f32[2,512,16,256]{3,2,1,0:T(8,128)}, f32[16,256]{1,0:T(8,128)S(1)}, f32[2,512,256]{2,1,0:T(8,128)}, f32[1,1,16,256]{3,2,1,0:T(8,128)S(1)}, /*index=5*/f32[1,16,256]{2,1,0:T(8,128)S(1)}, s32[]{:T(128)}) while((s32[]{:T(128)}, f32[2,512,16,256]{3,2,1,0:T(8,128)}, f32[16,256]{1,0:T(8,128)S(1)}, ...), condition=%wide.region_2.3_spmd, body=%wide.region_1.2_spmd.sunk | while | flops 824253504 | bytes 64828252 | solution.py:151
  31.4 2.5 copy.232
  33.9 113.5 %fusion.206 = f32[16,32,16,256]{1,0,3,2:T(8,128)} fusion(f32[32,32]{1,0:T(8,128)S(1)} %maximum_convert_fusion.4, f32[16,256]{1,0:T(8,128)S(1)} %bitcast.353, pred[32,32]{1,0:T(8,128)(4,1)S(1)} %fusion.205, f32[16,32,256]{1,0,2:T(8,128)} %copy.232, f32[16,256]{1,0:T(8,128)S(1)} %get-tuple-element.1020), kind=kOutput, calls=%fused_computation.74.clone.3 | convolution fusion | flops 815792128 | bytes 8950784 | tf_op jit(solution)/shard_map/while/body/eval_jaxpr/tsnc,gsnc->gtnc/dot_general | solution.py:86
  147.4 25.2 %slice.80 = f32[16,1,16,256]{1,0,3,2:T(8,128)} slice(f32[16,32,16,256]{1,0,3,2:T(8,128)} %fusion.206), slice={[0:16], [31:32], [0:16], [0:256]} | slice | bytes 524288 | tf_op jit(solution)/shard_map/while/body/eval_jaxpr/slice | solution.py:91
  172.6 15.7 %copy.233 = f32[16,1,16,256]{3,2,0,1:T(8,128)S(1)} copy(f32[16,1,16,256]{1,0,3,2:T(8,128)} %slice.80) | data formatting | bytes 524288 | tf_op jit(solution)/shard_map/while
  192.0 23.7 %multiply_add_fusion.9 = f32[16,32,16,256]{1,0,3,2:T(8,128)} fusion(f32[16,32,16,256]{1,0,3,2:T(8,128)} %fusion.206, f32[16,16,256]{0,2,1:T(8,128)} %bitcast.317, f32[32,16,256]{0,2,1:T(8,128)S(1)} %multiply_exponential_fusion.7), kind=kLoop, calls=%fused_computation.66.clone.1 | loop fusion | flops 4194304 | bytes 17563648 | tf_op jit(solution)/shard_map/while/body/eval_jaxpr/add | solution.py:103
  215.7 18.2 %copy.235 = f32[16,32,16,256]{3,2,1,0:T(8,128)} copy(f32[16,32,16,256]{1,0,3,2:T(8,128)} %multiply_add_fusion.9) | data formatting | bytes 16777216 | tf_op jit(solution)/shard_map/while/body/eval_jaxpr/add | solution.py:103
  233.9 7.7 bitcast_dynamic-update-slice_fusion.6
  242.7 2.5 copy.232
  245.1 113.5 %fusion.206 = f32[16,32,16,256]{1,0,3,2:T(8,128)} fusion(f32[32,32]{1,0:T(8,128)S(1)} %maximum_convert_fusion.4, f32[16,256]{1,0:T(8,128)S(1)} %bitcast.353, pred[32,32]{1,0:T(8,128)(4,1)S(1)} %fusion.205, f32[16,32,256]{1,0,2:T(8,128)} %copy.232, f32[16,256]{1,0:T(8,128)S(1)} %get-tuple-element.1020), kind=kOutput, calls=%fused_computation.74.clone.3 | convolution fusion | flops 815792128 | bytes 8950784 | tf_op jit(solution)/shard_map/while/body/eval_jaxpr/tsnc,gsnc->gtnc/dot_general | solution.py:86
  358.7 25.2 %slice.80 = f32[16,1,16,256]{1,0,3,2:T(8,128)} slice(f32[16,32,16,256]{1,0,3,2:T(8,128)} %fusion.206), slice={[0:16], [31:32], [0:16], [0:256]} | slice | bytes 524288 | tf_op jit(solution)/shard_map/while/body/eval_jaxpr/slice | solution.py:91
  383.8 15.7 %copy.233 = f32[16,1,16,256]{3,2,0,1:T(8,128)S(1)} copy(f32[16,1,16,256]{1,0,3,2:T(8,128)} %slice.80) | data formatting | bytes 524288 | tf_op jit(solution)/shard_map/while
  403.3 23.7 %multiply_add_fusion.9 = f32[16,32,16,256]{1,0,3,2:T(8,128)} fusion(f32[16,32,16,256]{1,0,3,2:T(8,128)} %fusion.206, f32[16,16,256]{0,2,1:T(8,128)} %bitcast.317, f32[32,16,256]{0,2,1:T(8,128)S(1)} %multiply_exponential_fusion.7), kind=kLoop, calls=%fused_computation.66.clone.1 | loop fusion | flops 4194304 | bytes 17563648 | tf_op jit(solution)/shard_map/while/body/eval_jaxpr/add | solution.py:103
  427.0 18.2 %copy.235 = f32[16,32,16,256]{3,2,1,0:T(8,128)} copy(f32[16,32,16,256]{1,0,3,2:T(8,128)} %multiply_add_fusion.9) | data formatting | bytes 16777216 | tf_op jit(solution)/shard_map/while/body/eval_jaxpr/add | solution.py:103
  445.2 7.7 bitcast_dynamic-update-slice_fusion.6
  453.4 32.3 %all-gather = f32[128,256]{1,0:T(8,128)S(1)} all-gather(f32[16,256]{1,0:T(8,128)S(1)} %copy-done.66), channel_id=4, replica_groups=mesh['seq'=8,'tensor'=4] {'seq'}, dimensions={0}, use_global_device_ids=true | all-gather | bytes 147456 | tf_op jit(solution)/shard_map/all_gather | solution.py:19
  486.4 30.7 %all-gather.1 = f32[16,1,16,256]{3,2,1,0:T(8,128)S(1)} all-gather(f32[2,1,16,256]{3,2,1,0:T(8,128)S(1)} %slice.48), channel_id=5, replica_groups=mesh['seq'=8,'tensor'=4] {'seq'}, dimensions={0}, use_global_device_ids=true | all-gather | bytes 294912 | tf_op jit(solution)/shard_map/all_gather | solution.py:19
  519.6 3.8 fusion.77
  523.5 7.3 all_gather.24
  536.7 3.3 convolution_convert_fusion.3
  545.7 15.3 %while.83 = (s32[]{:T(128)}, bf16[2,512,256]{1,2,0:T(8,128)(2,1)}, f32[2,2,512,1]{2,1,3,0:T(2,128)}, bf16[2,128,256]{1,2,0:T(8,128)(2,1)}, bf16[2,512,256]{1,2,0...) while((s32[]{:T(128)}, bf16[2,512,256]{1,2,0:T(8,128)(2,1)}, ...), condition=%wide.region_9.10_spmd, body=%wide.region_6.9_spmd.sunk | while | flops 344849408 | bytes 17334512 | solution.py:210
  561.0 3.3 convolution_convert_fusion
  564.6 51.6 %all-reduce.8.cloned.1.call-done = bf16[2,512,1024]{2,1,0:T(8,128)(2,1)} async-done(((bf16[2,512,1024]{2,1,0:T(8,128)(2,1)}), bf16[2,512,1024]{2,1,0:T(8,128)(2,1)}) %all-reduce.8.cloned.1.call-update) | async-done | bytes 2097168 | tf_op jit(solution)/shard_map/psum | solution.py:212
  616.3 5.0 convert_add_fusion.1
  622.0 3.3 fusion.110
  625.3 10.2 multiply_convert_fusion.3
  635.6 3.8 add_convert_fusion.2
  640.7 3.8 fusion.91
  644.8 51.3 %all-reduce.10.cloned.1.call-done = bf16[2,512,1024]{2,1,0:T(8,128)(2,1)} async-done(((bf16[2,512,1024]{2,1,0:T(8,128)(2,1)}), bf16[2,512,1024]{2,1,0:T(8,128)(2,1)}) %all-reduce.10.cloned.1.call-update) | async-done | bytes 2097168 | tf_op jit(solution)/shard_map/psum | solution.py:236
  696.1 3.6 multiply_reduce_fusion.6
  700.9 2.6 multiply_add_fusion.4
  709.7 23.7 %while.84 = (s32[]{:T(128)}, bf16[2,512,256]{1,2,0:T(8,128)(2,1)}, bf16[2,512,256]{1,2,0:T(8,128)(2,1)}, bf16[2,512,256]{1,2,0:T(8,128)(2,1)}, bf16[2,128,256]{1...) while((s32[]{:T(128)}, bf16[2,512,256]{1,2,0:T(8,128)(2,1)}, ...), condition=%wide.region_17.18_spmd, body=%wide.region_15.17_spmd.sunk | while | flops 847477760 | bytes 54415800 | solution.py:280
  715.5 3.1 multiply_reduce_fusion.15
  727.3 3.1 multiply_reduce_fusion.15
  737.2 6.0 fusion.94
  748.0 33.0 %all-gather.2 = bf16[128,256]{1,0:T(8,128)(2,1)} all-gather(bf16[16,256]{1,0:T(8,128)(2,1)S(1)} %copy-done.75), channel_id=6, replica_groups=mesh['seq'=8,'tensor'=4] {'seq'}, dimensions={0}, use_global_device_ids=true | all-gather | bytes 73728 | tf_op jit(solution)/shard_map/all_gather | solution.py:36
  781.0 7.0 multiply_exponential_fusion.2
  788.0 3.9 bitcast_convert_fusion
  791.9 3.8 bitcast_convert_fusion.1
  808.3 8.0 broadcast.478
  816.4 364.4 %while.85 = (s32[]{:T(128)}, f32[2,512,16,256]{3,2,1,0:T(8,128)}, f32[16,256]{1,0:T(8,128)S(1)}, f32[2,512,256]{2,1,0:T(8,128)S(1)}, f32[1,1,16,256]{3,2,1,0:T(8,128)S(1)}, /*index=5*/f32[1,16,256]{2,1,0:T(8,128)S(1)}, s32[]{:T(128)}) while((s32[]{:T(128)}, f32[2,512,16,256]{3,2,1,0:T(8,128)}, f32[16,256]{1,0:T(8,128)S(1)}, ...), condition=%wide.region_21.22_spmd, body=%wide.region_20.21_spmd.sunk | while | flops 824253504 | bytes 72692632 | solution.py:313
  818.9 112.2 %fusion.228 = f32[16,32,16,256]{1,0,3,2:T(8,128)} fusion(f32[32,32]{1,0:T(8,128)S(1)} %maximum_convert_fusion.5, f32[16,256]{1,0:T(8,128)S(1)} %bitcast.355, pred[32,32]{1,0:T(8,128)(4,1)S(1)} %fusion.227, f32[16,32,256]{1,0,2:T(8,128)S(1)} %copy.243, f32[16,256]{1,0:T(8,128)S(1)} %get-tuple-element.1137), kind=kOutput, calls=%fused_computation.99.clone.1 | convolution fusion | flops 815792128 | bytes 8950784 | tf_op jit(solution)/shard_map/while/body/eval_jaxpr/tsnc,gsnc->gtnc/dot_general | solution.py:86
  931.1 16.0 %copy.244 = f32[16,1,16,256]{3,2,0,1:T(8,128)S(1)} copy(f32[16,1,16,256]{1,0,3,2:T(8,128)} %bitcast.314) | data formatting | bytes 524288 | tf_op jit(solution)/shard_map/while
  949.5 23.1 %multiply_add_fusion.10 = f32[16,32,16,256]{1,0,3,2:T(8,128)} fusion(f32[16,32,16,256]{1,0,3,2:T(8,128)} %fusion.228, f32[16,16,256]{0,2,1:T(8,128)S(1)} %bitcast.318, f32[32,16,256]{0,2,1:T(8,128)S(1)} %multiply_exponential_fusion.8), kind=kLoop, calls=%fused_computation.91.clone.1 | loop fusion | flops 4194304 | bytes 17563648 | tf_op jit(solution)/shard_map/while/body/eval_jaxpr/add | solution.py:103
  972.6 18.6 %copy.246 = f32[16,32,16,256]{3,2,1,0:T(8,128)} copy(f32[16,32,16,256]{1,0,3,2:T(8,128)} %multiply_add_fusion.10) | data formatting | bytes 16777216 | tf_op jit(solution)/shard_map/while/body/eval_jaxpr/add | solution.py:103
  991.2 7.7 bitcast_dynamic-update-slice_fusion.8
  1001.2 112.2 %fusion.228 = f32[16,32,16,256]{1,0,3,2:T(8,128)} fusion(f32[32,32]{1,0:T(8,128)S(1)} %maximum_convert_fusion.5, f32[16,256]{1,0:T(8,128)S(1)} %bitcast.355, pred[32,32]{1,0:T(8,128)(4,1)S(1)} %fusion.227, f32[16,32,256]{1,0,2:T(8,128)S(1)} %copy.243, f32[16,256]{1,0:T(8,128)S(1)} %get-tuple-element.1137), kind=kOutput, calls=%fused_computation.99.clone.1 | convolution fusion | flops 815792128 | bytes 8950784 | tf_op jit(solution)/shard_map/while/body/eval_jaxpr/tsnc,gsnc->gtnc/dot_general | solution.py:86
  1113.4 15.7 %copy.244 = f32[16,1,16,256]{3,2,0,1:T(8,128)S(1)} copy(f32[16,1,16,256]{1,0,3,2:T(8,128)} %bitcast.314) | data formatting | bytes 524288 | tf_op jit(solution)/shard_map/while
  1131.5 23.1 %multiply_add_fusion.10 = f32[16,32,16,256]{1,0,3,2:T(8,128)} fusion(f32[16,32,16,256]{1,0,3,2:T(8,128)} %fusion.228, f32[16,16,256]{0,2,1:T(8,128)S(1)} %bitcast.318, f32[32,16,256]{0,2,1:T(8,128)S(1)} %multiply_exponential_fusion.8), kind=kLoop, calls=%fused_computation.91.clone.1 | loop fusion | flops 4194304 | bytes 17563648 | tf_op jit(solution)/shard_map/while/body/eval_jaxpr/add | solution.py:103
  1154.6 18.2 %copy.246 = f32[16,32,16,256]{3,2,1,0:T(8,128)} copy(f32[16,32,16,256]{1,0,3,2:T(8,128)} %multiply_add_fusion.10) | data formatting | bytes 16777216 | tf_op jit(solution)/shard_map/while/body/eval_jaxpr/add | solution.py:103
  1172.8 7.8 bitcast_dynamic-update-slice_fusion.8
  1181.6 30.5 %all_gather.28 = bf16[8,2,16,256]{3,2,1,0:T(8,128)(2,1)S(1)} all-gather(bf16[1,2,16,256]{3,2,1,0:T(8,128)(2,1)S(1)} %fusion.131), channel_id=1, replica_groups=mesh['seq'=8,'tensor'=4] {'seq'}, dimensions={0}, use_global_device_ids=true | all-gather | bytes 147456 | tf_op jit(solution)/shard_map/all_gather | solution.py:36
  1212.1 14.2 %multiply_reduce_fusion.3 = (bf16[16,256]{1,0:T(8,128)(2,1)S(1)}, f32[2,512,16,256]{3,2,1,0:T(8,128)}) fusion(f32[2,512,256]{2,1,0:T(8,128)S(1)} %get-tuple-element.1217, f32[2,512,16,256]{3,2,1,0:T(8,128)} %get-tuple-element.460, f32[2,16,256]{2,1,0:T(8,128)S(1)} %copy-done.33, f32[512,16,256]{2,1,0:T(8,128)} %get-tuple-element.691), kind=kLoop, calls=%fused_computation.114 | loop fusion | flops 16773120 | bytes 43032576 | tf_op jit(solution)/shard_map/reduce_sum | solution.py:321
  1226.3 2.4 add_convert_fusion.4
  1229.1 13.8 %slice.62 = f32[2,511,16,256]{3,2,1,0:T(8,128)} slice(f32[2,512,16,256]{3,2,1,0:T(8,128)} %get-tuple-element.668), slice={[0:2], [0:511], [0:16], [0:256]} | slice | bytes 33488896 | tf_op jit(solution)/shard_map/slice | solution.py:318
  1246.5 17.7 %multiply_reduce_fusion.4 = (f32[16,256]{1,0:T(8,128)S(1)}, f32[16,256]{1,0:T(8,128)S(1)}, f32[2,512,256]{2,1,0:T(8,128)S(1)}) fusion(f32[2,512,16,256]{3,2,1,0:T(8,128)S(1)} %bitcast.321, f32[2,512,256]{2,1,0:T(8,128)S(1)} %copy-done.12, f32[2,16,256]{2,1,0:T(8,128)S(1)} %get-tuple-element.470, f32[512,16,256]{2,1,0:T(8,128)} %get-tuple-element.692, ...), kind=kLoop, calls=%fused_computation.116 | loop fusion | flops 37478400 | bytes 44122112 | tf_op jit(solution)/shard_map/reduce_sum | solution.py:320
  1266.5 5.8 all-reduce.1
  1272.3 37.1 %all-reduce.2 = (bf16[256]{0:T(256)(128)(2,1)S(1)}, bf16[1024]{0:T(1024)(128)(2,1)S(1)}, bf16[16,256]{1,0:T(8,128)(2,1)S(1)}, bf16[16,256]{1,0:T(8,128)(2,1)S(1)...) all-reduce(bf16[256]{0:T(256)(128)(2,1)S(1)} %get-tuple-element.559, ...), channel_id=1, replica_groups=mesh['seq'=8,'tensor'=4] {'seq'}, use_global_device_ids=true, to_apply=%region_28.29 | all-reduce | flops 13824 | bytes 55296 | tf_op jit(solution)/shard_map/psum | solution.py:341
  1312.9 2.7 add_convert_fusion.3
  1323.1 2.5 convert_element_type.366
  1325.6 2.5 convert_element_type.368
  1328.1 3.1 copy.316
  (437 shorter events, 124.3 us)
Async XLA Ops:
  7.2 614.7 %copy-start = (bf16[1024,1024]{1,0:T(8,128)(2,1)S(1)}, bf16[1024,1024]{1,0:T(8,128)(2,1)}, u32[]{:S(2)}) copy-start(bf16[1024,1024]{1,0:T(8,128)(2,1)} %param.36) | copy-start | bytes 6291460
  7.2 609.1 %all-reduce.8.cloned.1.call-start = ((), (), s32[]{:S(2)}) async-start(), calls=%async_computation.3 | async-start | bytes 4194304 | tf_op jit(solution)/shard_map/psum | solution.py:212
  17.4 4.1 copy-start.62
  17.4 4.1 copy-start.64
  30.1 423.2 %copy-start.66 = (f32[16,256]{1,0:T(8,128)S(1)}, f32[16,256]{1,0:T(8,128)}, u32[]{:S(2)}) copy-start(f32[16,256]{1,0:T(8,128)} %get-tuple-element.697) | copy-start | bytes 49156
  30.1 487.1 %copy-start.31 = (f32[2,16,256]{2,1,0:T(8,128)S(1)}, f32[2,16,256]{2,1,0:T(8,128)}, u32[]{:S(2)}) copy-start(f32[2,16,256]{2,1,0:T(8,128)} %custom-call) | copy-start | bytes 98308
  30.1 489.1 %copy-start.59 = (f32[16,256]{1,0:T(8,128)S(1)}, f32[16,256]{1,0:T(8,128)}, u32[]{:S(2)}) copy-start(f32[16,256]{1,0:T(8,128)} %get-tuple-element.698) | copy-start | bytes 49156
  453.3 70.1 %copy-start.50 = (f32[1,16,256]{2,1,0:T(8,128)}, f32[1,16,256]{2,1,0:T(8,128)S(1)}, u32[]{:S(2)}) copy-start(f32[1,16,256]{2,1,0:T(8,128)S(1)} %get-tuple-element.1245) | copy-start | bytes 49156
  453.3 70.1 %copy-start.60 = (f32[16,256]{1,0:T(8,128)}, f32[16,256]{1,0:T(8,128)S(1)}, u32[]{:S(2)}) copy-start(f32[16,256]{1,0:T(8,128)S(1)} %get-tuple-element.1254) | copy-start | bytes 49156
  453.3 70.1 %copy-start.80 = (f32[1,1,16,256]{3,2,1,0:T(8,128)}, f32[1,1,16,256]{3,2,1,0:T(8,128)S(1)}, u32[]{:S(2)}) copy-start(f32[1,1,16,256]{3,2,1,0:T(8,128)S(1)} %get-tuple-element.1255) | copy-start | bytes 49156
  453.3 66.3 %copy-start.76 = (f32[16,256]{1,0:T(8,128)S(1)}, f32[16,256]{1,0:T(8,128)}, u32[]{:S(2)}) copy-start(f32[16,256]{1,0:T(8,128)} %param.40) | copy-start | bytes 49156
  517.5 5.9 copy-start.32
  519.2 4.2 copy-start.85
  519.5 11.3 copy-start.8
  519.6 11.3 copy-start.22
  519.6 11.3 copy-start.72
  519.6 11.3 copy-start.83
  523.4 9.3 copy-start.24
  536.7 8.2 copy-start.52
  564.3 131.9 %all-reduce.10.cloned.1.call-start = ((), (), s32[]{:S(2)}) async-start(), calls=%async_computation.6 | async-start | bytes 4194304 | tf_op jit(solution)/shard_map/psum | solution.py:236
  616.3 5.0 copy-start.9
  616.3 5.0 copy-start.21
  625.3 10.3 copy-start.47
  625.3 10.3 copy-start.89
  644.5 161.7 %reduce-scatter.8.cloned.1.call-start = ((), (), s32[]{:S(2)}) async-start(), calls=%async_computation.8 | async-start | bytes 655360 | tf_op jit(solution)/shard_map/reduce_scatter | solution.py:302
  696.1 4.1 copy-start.6
  696.1 4.7 copy-start.17
  700.9 4.7 copy-start.46
  705.6 4.1 copy-start.29
  705.6 4.1 copy-start.30
  705.6 4.1 copy-start.70
  737.1 489.2 %reduce-scatter.4.cloned.1.call-start = ((), (), s32[]{:S(2)}) async-start(), calls=%async_computation.4 | async-start | bytes 2621440 | tf_op jit(solution)/shard_map/reduce_scatter | solution.py:220
  737.2 6.1 copy-start.38
  737.2 6.1 copy-start.53
  743.2 521.1 %reduce-scatter.6.cloned.1.call-start = ((), (), s32[]{:S(2)}) async-start(), calls=%async_computation.7 | async-start | bytes 2621440 | tf_op jit(solution)/shard_map/reduce_scatter | solution.py:327
  747.3 568.3 %all-reduce.12.cloned.1.call-start = ((), (), s32[]{:S(2)}) async-start(), calls=%async_computation.9 | async-start | bytes 12582912 | tf_op jit(solution)/shard_map/psum | solution.py:342
  781.0 7.0 copy-start.48
  781.0 7.0 copy-start.49
  788.0 3.9 copy-start.7
  806.2 521.9 %all-gather.5.cloned.1.call-start = ((), (), s32[]{:S(2)}) async-start(), calls=%async_computation.5 | async-start | bytes 2621440 | tf_op jit(solution)/shard_map/all_gather | solution.py:223
  808.3 8.1 copy-start.51
  808.3 8.1 copy-start.77
  808.3 8.1 copy-start.81
  816.4 364.4 %copy-start.67 = (f32[16,256]{1,0:T(8,128)S(1)}, f32[16,256]{1,0:T(8,128)}, u32[]{:S(2)}) copy-start(f32[16,256]{1,0:T(8,128)} %get-tuple-element.693) | copy-start | bytes 49156
  816.4 395.7 %copy-start.33 = (f32[2,16,256]{2,1,0:T(8,128)S(1)}, f32[2,16,256]{2,1,0:T(8,128)}, u32[]{:S(2)}) copy-start(f32[2,16,256]{2,1,0:T(8,128)} %copy-done.32) | copy-start | bytes 98308
  991.2 7.7 copy-start.14
  1172.8 7.8 copy-start.14
  1180.8 45.5 %copy-start.15 = (f32[2,512,256]{2,1,0:T(8,128)}, f32[2,512,256]{2,1,0:T(8,128)S(1)}, u32[]{:S(2)}) copy-start(f32[2,512,256]{2,1,0:T(8,128)S(1)} %get-tuple-element.1217) | copy-start | bytes 3145732
  1212.1 16.6 %copy-start.58 = (bf16[128,256]{1,0:T(8,128)(2,1)S(1)}, bf16[128,256]{1,0:T(8,128)(2,1)}, u32[]{:S(2)}) copy-start(bf16[128,256]{1,0:T(8,128)(2,1)} %all-gather.2) | copy-start | bytes 196612
  1229.1 13.9 %slice-start = ((s8[16777216]{0:T(1024)(128)(4,1)}), s8[4194304]{0:T(1024)(128)(4,1)S(1)}, s32[]{:S(2)}) async-start(s8[16777216]{0:T(1024)(128)(4,1)} %bitcast.320), calls=%async_computation.10 | async-start | bytes 8388608
  1229.1 14.3 %slice-start.1 = ((s8[16777216]{0:T(1024)(128)(4,1)}), s8[4194304]{0:T(1024)(128)(4,1)S(1)}, s32[]{:S(2)}) async-start(s8[16777216]{0:T(1024)(128)(4,1)} %bitcast.320), calls=%async_computation.11 | async-start | bytes 8388608
  1229.1 15.9 %slice-start.2 = ((s8[16777216]{0:T(1024)(128)(4,1)}), s8[4194304]{0:T(1024)(128)(4,1)S(1)}, s32[]{:S(2)}) async-start(s8[16777216]{0:T(1024)(128)(4,1)} %bitcast.320), calls=%async_computation.12 | async-start | bytes 8388608
  1229.1 17.1 %slice-start.3 = ((s8[16777216]{0:T(1024)(128)(4,1)}), s8[4194304]{0:T(1024)(128)(4,1)S(1)}, s32[]{:S(2)}) async-start(s8[16777216]{0:T(1024)(128)(4,1)} %bitcast.320), calls=%async_computation.13 | async-start | bytes 8388608
  1229.1 17.3 %copy-start.12 = (f32[2,512,256]{2,1,0:T(8,128)S(1)}, f32[2,512,256]{2,1,0:T(8,128)}, u32[]{:S(2)}) copy-start(f32[2,512,256]{2,1,0:T(8,128)} %get-tuple-element.1216) | copy-start | bytes 3145732
  1229.1 17.3 %copy-start.61 = (f32[16,256]{1,0:T(8,128)S(1)}, f32[16,256]{1,0:T(8,128)}, u32[]{:S(2)}) copy-start(f32[16,256]{1,0:T(8,128)} %copy-done.60) | copy-start | bytes 49156
  1246.5 17.7 %copy-start.63 = (f32[16,256]{1,0:T(8,128)S(1)}, f32[16,256]{1,0:T(8,128)}, u32[]{:S(2)}) copy-start(f32[16,256]{1,0:T(8,128)} %param.38) | copy-start | bytes 49156
  1246.5 17.7 %copy-start.65 = (f32[16,256]{1,0:T(8,128)S(1)}, f32[16,256]{1,0:T(8,128)}, u32[]{:S(2)}) copy-start(f32[16,256]{1,0:T(8,128)} %param.39) | copy-start | bytes 49156
  1246.5 17.8 %copy-start.16 = (f32[2,512,256]{2,1,0:T(8,128)S(1)}, f32[2,512,256]{2,1,0:T(8,128)}, u32[]{:S(2)}) copy-start(f32[2,512,256]{2,1,0:T(8,128)} %copy-done.15) | copy-start | bytes 3145732
  1246.5 17.8 %copy-start.82 = (f32[256]{0:T(256)S(1)}, f32[256]{0:T(256)}, u32[]{:S(2)}) copy-start(f32[256]{0:T(256)} %dynamic_slice.102) | copy-start | bytes 3076
  1246.5 17.8 %copy-start.86 = (f32[256]{0:T(256)S(1)}, f32[256]{0:T(256)}, u32[]{:S(2)}) copy-start(f32[256]{0:T(256)} %param.41) | copy-start | bytes 3076
  1264.2 48.7 %copy-start.74 = (f32[2,512]{1,0:T(2,128)S(1)}, f32[2,512]{1,0:T(2,128)}, u32[]{:S(2)}) copy-start(f32[2,512]{1,0:T(2,128)} %copy-done.71) | copy-start | bytes 12292
  1315.6 6.4 copy-start.54
  1315.6 7.5 copy-start.35
  1325.6 5.6 copy-start.1
  (54 other events, 90.3 us)
Sparse Core Ops, SparseCore 0:
  564.4 51.8 all-reduce.7
  644.7 51.4 all-reduce.9
  737.2 21.7 reduce-scatter.7
  761.5 31.3 reduce-scatter.3
  795.3 31.4 reduce-scatter.5
  833.1 216.2 all-reduce.11
  1228.9 22.5 all-gather.4
where the time goes:
time: 1340 us
  matrix products  521 us (39%)
  local copies, waits for them, and re-layouts  314 us (23%)
  other arithmetic  205 us (15%)
  blocking collectives  177 us (13%)
  waiting for transfers between devices  103 us (8%)
  between operations  15.4 us (1%)
    dot_general x4, matrix products, run_states(): jnp.einsum('tsnc,gsnc->gtnc', power_table(rate, inner_lag), pieces, preci...  451 us
    add x4, other arithmetic, run_states(): full = inner + reach_pow[None] * entering[:, None]  93.7 us
    add x4, local copies, waits for them, and re-layouts, run_states(): full = inner + reach_pow[None] * entering[:, None]  73.1 us
    while x64, local copies, waits for them, and re-layouts  68.4 us
    all_gather x2, blocking collectives, carried_in(): lax.all_gather(a.astype(kind), axis)  63.5 us
    all_gather x2, blocking collectives, entering_2(): pieces = jax.tree.map(lambda part: lax.all_gather(part, axis), value)  63 us
    psum x1, waiting for transfers between devices, local(): lax.psum(attn_part.astype(jnp.bfloat16), 'tensor').astype(jnp.float32)  51.6 us
    psum x1, waiting for transfers between devices, local(): lax.psum(n2_part.astype(jnp.bfloat16), 'tensor').astype(jnp.float32)  51.3 us
  transfers between devices with their start and end apart: 7, of which 2 were waited for; matrix products, arithmetic and copies ran while one was open for 36% of the time, Pallas kernels for 0%

commit v1 on v0

v1 whole, which is shorter than its diff:
```python
import functools

import jax
import jax.numpy as jnp
from jax import lax
from jax.experimental import pallas as pl
from jax.experimental.pallas import tpu as pltpu
from jax.sharding import PartitionSpec as P

HD = 128
NS = 16
CTX = 128
SUB = 8
EPS = 1e-06
F32 = jnp.float32
BF16 = jnp.bfloat16
MIB = 1 << 20


def nn(a, b):
    return lax.dot_general(a, b, (((1,), (0,)), ((), ())), preferred_element_type=F32)


def nt(a, b):
    return lax.dot_general(a, b, (((1,), (1,)), ((), ())), preferred_element_type=F32)


def tn(a, b):
    return lax.dot_general(a, b, (((0,), (0,)), ((), ())), preferred_element_type=F32)


def swap(value, axis, bit):
    count = lax.axis_size(axis)
    return lax.ppermute(value, axis, [(i, i ^ bit) for i in range(count)])


def low_bits(count):
    bit, out = 1, []
    while bit < count:
        out.append(bit)
        bit *= 2
    return out


def sds(shape, dtype):
    return jax.ShapeDtypeStruct(shape, dtype)


def vmem():
    return pl.BlockSpec(memory_space=pltpu.VMEM)


def smem():
    return pl.BlockSpec(memory_space=pltpu.SMEM)


def params(limit_mib, sems=None):
    return pltpu.CompilerParams(vmem_limit_bytes=limit_mib * MIB, dimension_semantics=sems)


def cost(flops, nbytes, trans=0):
    return pl.CostEstimate(flops=int(flops), bytes_accessed=int(nbytes), transcendentals=int(trans))


def lanes(tile):
    return slice(tile * HD, (tile + 1) * HD)


def spread(table, rows, factor=None):
    for n in range(NS):
        row = rows[n : n + 1, :]
        if factor is not None:
            row = jnp.exp(row * factor)
        table[n] = jnp.broadcast_to(row, table.shape[1:])


def scan_step(hat_ref, decay_tab, jump_tab, group, state, stride, seg):
    tiles = hat_ref.shape[0]
    taps = [[hat_ref[t, pl.ds(group * stride + i, SUB, stride=seg), :] for i in range(stride)] for t in range(tiles)]
    out = []
    for n in range(NS):
        for t in range(tiles):
            decay = decay_tab[n, :, lanes(t)]
            inner = taps[t][0]
            for tap in taps[t][1:]:
                inner = inner * decay + tap
            out.append(state[n * tiles + t] * jump_tab[n, :, lanes(t)] + inner)
    return tuple(out), taps


def segment_ends(state, rate, seg, seqs, seg_ref, end_ref, forward):
    per = SUB // seqs
    tiles = rate.shape[1] // HD
    place = lax.rem(lax.broadcasted_iota(jnp.int32, (SUB, HD), 0), per)
    away = ((per - 1 - place if forward else place) * seg).astype(F32)
    for n in range(NS):
        for t in range(tiles):
            now = state[n * tiles + t]
            seg_ref[n, :, lanes(t)] = now
            part = now * jnp.exp(-rate[n : n + 1, lanes(t)] * away)
            for s in range(seqs):
                end_ref[s, n : n + 1, lanes(t)] = jnp.sum(part[s * per : (s + 1) * per], 0, keepdims=True)


def entry_states(entry_ref, carry_ref, seg_ref, hop, seqs, forward):
    per = SUB // seqs
    for n in range(NS):
        step = hop[n : n + 1, :]
        for s in range(seqs):
            now = carry_ref[s, n : n + 1, :]
            for k in range(per):
                q = s * per + (k if forward else per - 1 - k)
                entry_ref[n, q : q + 1, :] = now
                if k < per - 1:
                    now = now * step + seg_ref[n, q : q + 1, :]


def read_state(ref):
    tiles = ref.shape[2] // HD
    return tuple(ref[n, :, lanes(t)] for n in range(NS) for t in range(tiles))


def enter_kernel(seqs, stride, x_ref, xc_ref, gain_ref, rate_ref, low_ref, hat_ref, inv_ref, seg_ref, fin_ref, decay_tab, jump_tab):
    rows, width = x_ref.shape
    seg = rows // SUB
    tiles = hat_ref.shape[0]
    step = 64
    gain = gain_ref[...]

    def norm(i, carry):
        at = pl.ds(pl.multiple_of(i * step, step), step)
        x = x_ref[at, :].astype(F32)
        inv = lax.rsqrt(jnp.sum(x * x, -1, keepdims=True) * (1.0 / width) + EPS)
        low_ref[at, :] = (x * inv * gain).astype(BF16)
        inv_ref[at, :] = inv
        for t in range(tiles):
            hat_ref[t, at, :] = xc_ref[at, lanes(t)].astype(F32) * inv
        return carry

    lax.fori_loop(0, rows // step, norm, 0)
    rate = rate_ref[...]
    spread(decay_tab, rate, -1.0)
    spread(jump_tab, rate, -float(stride))

    def group(g, state):
        return scan_step(hat_ref, decay_tab, jump_tab, g, state, stride, seg)[0]

    state = lax.fori_loop(0, seg // stride, group, (jnp.zeros((SUB, HD), F32),) * (NS * tiles))
    segment_ends(state, rate, seg, seqs, seg_ref, fin_ref, True)


def context_kernel(seqs, stride, hat_ref, seg_ref, carry_ref, rate_ref, coeff_ref, sout_ref, skip_ref, gain_ref, ctx_ref, entry_ref, decay_tab, jump_tab, out_tab, flat):
    tiles = hat_ref.shape[0]
    seg = hat_ref.shape[1] // SUB
    rate = rate_ref[...]
    spread(decay_tab, rate, -1.0)
    spread(jump_tab, rate, -float(stride))
    spread(out_tab, coeff_ref[...] * sout_ref[...] * gain_ref[...])
    entry_states(entry_ref, carry_ref, seg_ref, jnp.exp(rate * (-float(seg))), seqs, True)
    skip = skip_ref[...] * gain_ref[...]
    groups = seg // stride

    def group(g, state):
        state, taps = scan_step(hat_ref, decay_tab, jump_tab, g, state, stride, seg)
        for t in range(tiles):
            total = skip[:, lanes(t)] * taps[t][-1]
            for n in range(NS):
                total = total + out_tab[n, :, lanes(t)] * state[n * tiles + t]
            flat[t, pl.ds(g, SUB, stride=groups), :] = total
        return state

    lax.fori_loop(0, groups, group, read_state(entry_ref))
    for t in range(tiles):
        ctx_ref[:, lanes(t)] = flat[t].astype(BF16)


def lead_kernel(seqs, stride, near_ref, far_ref, rate_ref, grad_ref, segb_ref, lead_ref, jump_tab):
    tiles = grad_ref.shape[0]
    groups = grad_ref.shape[1] // SUB
    for t in range(tiles):
        grad_ref[t] = near_ref[:, lanes(t)].astype(F32) + far_ref[:, lanes(t)].astype(F32)
    rate = rate_ref[...]
    spread(jump_tab, rate, -float(stride))

    def group(i, state):
        g = groups - 1 - i
        grads = [grad_ref[t, pl.ds(g, SUB, stride=groups), :] for t in range(tiles)]
        return tuple(state[n * tiles + t] * jump_tab[n, :, lanes(t)] + grads[t] for n in range(NS) for t in range(tiles))

    state = lax.fori_loop(0, groups, group, (jnp.zeros((SUB, HD), F32),) * (NS * tiles))
    segment_ends(state, rate, groups * stride, seqs, segb_ref, lead_ref, False)


def state_back_kernel(
    seqs, stride, hat_ref, grad_ref, entry_ref, segb_ref, carryb_ref, rate_ref, root_ref, sin_ref, sout_ref, skip_ref, gain_ref,
    back_ref, rateg_ref, sing_ref, soutg_ref, skipg_ref,
    decay_tab, jump_tab, tap_tab, entryb, states, sums,
):
    tiles = hat_ref.shape[0]
    seg = hat_ref.shape[1] // SUB
    groups = seg // stride
    rate = rate_ref[...]
    root = root_ref[...]
    s_in = sin_ref[...]
    s_out = sout_ref[...]
    gain = gain_ref[...]
    coeff = root * s_in
    spread(decay_tab, rate, -1.0)
    spread(jump_tab, rate, -float(stride))
    both = coeff * s_out
    for i in range(stride):
        spread(tap_tab.at[i], both * jnp.exp(rate * (-float(stride - 1 - i))))
    entry_states(entryb, carryb_ref, segb_ref, jnp.exp(rate * (-float(seg))), seqs, False)
    skip = skip_ref[...]

    def forward(g, state):
        for n in range(NS):
            for t in range(tiles):
                states[g, n, :, lanes(t)] = state[n * tiles + t]
        return scan_step(hat_ref, decay_tab, jump_tab, g, state, stride, seg)[0]

    last = lax.fori_loop(0, groups, forward, read_state(entry_ref))
    for n in range(NS):
        for t in range(tiles):
            states[groups, n, :, lanes(t)] = last[n * tiles + t]
    zero = jnp.zeros((SUB, HD), F32)

    def span(g, i):
        return pl.ds(g * stride + i, SUB, stride=seg)

    for t in range(tiles):

        def skips(g, total, t=t):
            grad = grad_ref[t, pl.ds(g, SUB, stride=groups), :]
            for i in range(stride - 1):
                back_ref[t, span(g, i), :] = zero
            back_ref[t, span(g, stride - 1), :] = grad * skip[:, lanes(t)]
            return total + grad * hat_ref[t, span(g, stride - 1), :]

        total = lax.fori_loop(0, groups, skips, zero)
        skipg_ref[:, lanes(t)] = jnp.sum(total, 0, keepdims=True) * gain[:, lanes(t)]
    lot = 4
    kinds = stride + 2
    for t in range(tiles):
        for first in range(0, NS, lot):
            names = range(first, first + lot)

            def group(i, carry, t=t, names=names):
                g = groups - 1 - i
                adj, acc = carry
                grad = grad_ref[t, pl.ds(g, SUB, stride=groups), :]
                taps = [hat_ref[t, span(g, i), :] for i in range(stride)]
                backs = [back_ref[t, span(g, i), :] for i in range(stride)]
                new_adj, new_acc = [], []
                for k, n in enumerate(names):
                    now = adj[k] * jump_tab[n, :, lanes(t)] + grad
                    new_adj.append(now)
                    for i in range(stride):
                        backs[i] = backs[i] + tap_tab[i, n, :, lanes(t)] * now
                        new_acc.append(acc[k * kinds + i] + now * taps[i])
                    new_acc.append(acc[k * kinds + stride] + now * states[g, n, :, lanes(t)])
                    new_acc.append(acc[k * kinds + stride + 1] + grad * states[g + 1, n, :, lanes(t)])
                for i in range(stride):
                    back_ref[t, span(g, i), :] = backs[i]
                return tuple(new_adj), tuple(new_acc)

            start = (tuple(entryb[n, :, lanes(t)] for n in names), (zero,) * (lot * kinds))
            _, acc = lax.fori_loop(0, groups, group, start)
            for k, n in enumerate(names):
                for j in range(kinds):
                    sums[j, n : n + 1, lanes(t)] = jnp.sum(acc[k * kinds + j], 0, keepdims=True)
    decay = jnp.exp(-rate)
    powers = [jnp.ones_like(rate)]
    for _ in range(stride):
        powers.append(powers[-1] * decay)
    coeff_grad = sum(powers[stride - 1 - i] * sums[i] for i in range(stride)) * s_out * gain
    decay_grad = float(stride) * powers[stride - 1] * sums[stride]
    for i in range(stride - 1):
        decay_grad = decay_grad + float(stride - 1 - i) * powers[stride - 2 - i] * sums[i]
    decay_grad = decay_grad * coeff * s_out * gain
    soutg_ref[...] = coeff * gain * sums[stride + 1]
    sing_ref[...] = coeff_grad * root
    rateg_ref[...] = coeff_grad * s_in * (decay * decay / root) - decay * decay_grad


def carried(value, hop, axis, forward):
    count = lax.axis_size(axis)
    mine = lax.axis_index(axis)
    whole = value
    enter = jnp.zeros_like(value)
    for bit in low_bits(count):
        other = swap(whole, axis, bit)
        upper = (mine & bit) != 0
        offset = mine & (bit - 1)
        if not forward:
            upper = jnp.logical_not(upper)
            offset = bit - 1 - offset
        enter = jnp.where(upper, enter + hop(offset) * other, enter)
        span = hop(bit)
        whole = jnp.where(upper, whole + span * other, other + span * whole)
    return enter


def qkv_kernel(x_ref, wq_ref, wk_ref, wv_ref, q_ref, k_ref, v_ref):
    x = x_ref[...]
    q_ref[...] = nn(x, wq_ref[...]).astype(BF16)
    k_ref[...] = nn(x, wk_ref[...]).astype(BF16)
    v_ref[...] = nn(x, wv_ref[...]).astype(BF16)


def masks(first, tile, block, stride):
    row = lax.broadcasted_iota(jnp.int32, (tile, CTX), 0) + first
    col = lax.broadcasted_iota(jnp.int32, (tile, CTX), 1)
    side = stride * col + (stride - 1) <= row
    row = lax.broadcasted_iota(jnp.int32, (tile, block), 0) + first
    col = lax.broadcasted_iota(jnp.int32, (tile, block), 1)
    return side, col <= row


def attend_kernel(parts, scale, idx_ref, q_ref, k_ref, v_ref, wk_ref, wv_ref, *rest):
    ctx_refs, (out_ref, kc_ref, vc_ref, lse_ref) = rest[:parts], rest[parts:]
    block, width = q_ref.shape
    stride = block // CTX
    idx = idx_ref[0]
    key_c = jnp.zeros((CTX, width), F32)
    val_c = jnp.zeros((CTX, width), F32)
    for p in range(parts):
        at = pl.ds(pl.multiple_of((idx ^ p) * width, width), width)
        key_c = key_c + nn(ctx_refs[p][...], wk_ref[at, :])
        val_c = val_c + nn(ctx_refs[p][...], wv_ref[at, :])
    kc_ref[...] = key_c.astype(BF16)
    vc_ref[...] = val_c.astype(BF16)
    tile = min(256, block)
    for h in range(width // HD):
        cols = slice(h * HD, (h + 1) * HD)
        for first in range(0, block, tile):
            seen = first + tile
            rows = slice(first, seen)
            q = q_ref[rows, cols]
            side_ok, own_ok = masks(first, tile, seen, stride)
            side = jnp.where(side_ok, nt(q, kc_ref[:, cols]), -1e30)
            own = jnp.where(own_ok, nt(q, k_ref[:seen, cols]), -1e30)
            top = jnp.maximum(jnp.max(side, -1, keepdims=True), jnp.max(own, -1, keepdims=True))
            side = jnp.exp((side - top) * scale)
            own = jnp.exp((own - top) * scale)
            total = jnp.sum(side, -1, keepdims=True) + jnp.sum(own, -1, keepdims=True)
            share = 1.0 / total
            got = nn((side * share).astype(BF16), vc_ref[:, cols]) + nn((own * share).astype(BF16), v_ref[:seen, cols])
            out_ref[rows, cols] = got.astype(BF16)
            lse_ref[rows, h : h + 1] = top * scale + jnp.log(total)


def attend_back_kernel(
    seq, scale, info_ref, mid_ref, near_ref, far_ref, grad_ref, gain_ref, wo_ref, q_ref, k_ref, v_ref, kc_ref, vc_ref, lse_ref,
    wq_ref, wk_ref, wv_ref,
    low_ref, slice_ref, gaing_ref, dq_ref, dk_ref, dv_ref, dkc_ref, dvc_ref, ckeep_ref, csend_ref, nkeep_ref, nsend_ref,
    n2_ref, full_ref, key_acc, val_acc, skey_acc, sval_acc,
):
    block, width = q_ref.shape
    model = mid_ref.shape[1]
    half = model // 2
    stride = block // CTX
    idx, mine, limit = info_ref[0], info_ref[1], info_ref[2 + seq]
    n2_ref[:, pl.ds(pl.multiple_of(mine * half, half), half)] = near_ref[...]
    n2_ref[:, pl.ds(pl.multiple_of((1 - mine) * half, half), half)] = far_ref[...]
    gain = gain_ref[...]
    step = 64

    def norm(i, total):
        at = pl.ds(pl.multiple_of(i * step, step), step)
        mid = mid_ref[at, :]
        inv = lax.rsqrt(jnp.sum(mid * mid, -1, keepdims=True) * (1.0 / model) + EPS)
        hat = mid * inv
        n2 = n2_ref[at, :].astype(F32)
        prod = n2 * hat
        h2 = n2 * gain
        mean = jnp.sum(h2 * hat, -1, keepdims=True) * (1.0 / model)
        place = lax.broadcasted_iota(jnp.int32, (step, 1), 0) + i * step
        cot = jnp.where(place < limit, grad_ref[at, :].astype(F32), 0.0)
        grad = cot + inv * (h2 - hat * mean)
        full_ref[at, :] = grad
        low_ref[at, :] = grad.astype(BF16)
        return total + jnp.sum(prod, 0, keepdims=True)

    gaing_ref[...] = lax.fori_loop(0, block // step, norm, jnp.zeros((1, model), F32))
    slice_ref[...] = full_ref[:, pl.ds(pl.multiple_of(idx * width, width), width)]
    att_grad = nt(low_ref[...], wo_ref[...]).astype(BF16)
    tile = min(256, block)
    for h in range(width // HD):
        cols = slice(h * HD, (h + 1) * HD)
        for first in range(0, block, tile):
            seen = first + tile
            rows = slice(first, seen)
            q = q_ref[rows, cols]
            grad = att_grad[rows, cols]
            lse = lse_ref[rows, h : h + 1]
            side_ok, own_ok = masks(first, tile, seen, stride)
            kc, k = kc_ref[:, cols], k_ref[:seen, cols]
            side = jnp.exp(jnp.where(side_ok, nt(q, kc) * scale - lse, -1e30))
            own = jnp.exp(jnp.where(own_ok, nt(q, k) * scale - lse, -1e30))
            dside = nt(grad, vc_ref[:, cols])
            down = nt(grad, v_ref[:seen, cols])
            term = jnp.sum(side * dside, -1, keepdims=True) + jnp.sum(own * down, -1, keepdims=True)
            dside = (side * (dside - term)).astype(BF16)
            down = (own * (down - term)).astype(BF16)
            dq_ref[rows, cols] = ((nn(dside, kc) + nn(down, k)) * scale).astype(BF16)
            side = side.astype(BF16)
            own = own.astype(BF16)
            last = first + tile >= block
            fresh = first == 0
            for acc, score, right in (
                (skey_acc, dside, q),
                (sval_acc, side, grad),
            ):
                got = tn(score, right)
                acc[...] = got if fresh else acc[...] + got
            for acc, score, right in (
                (key_acc, down, q),
                (val_acc, own, grad),
            ):
                got = tn(score, right)
                if fresh:
                    acc[:seen, :] = got
                else:
                    acc[:first, :] = acc[:first, :] + got[:first]
                    acc[first:seen, :] = got[first:]
            if last:
                dk_ref[:, cols] = (key_acc[...] * scale).astype(BF16)
                dv_ref[:, cols] = val_acc[...].astype(BF16)
                dkc_ref[:, cols] = (skey_acc[...] * scale).astype(BF16)
                dvc_ref[:, cols] = sval_acc[...].astype(BF16)
    count = model // width
    for p in range(count):
        at = pl.ds(pl.multiple_of((idx ^ p) * width, width), width)
        wk, wv = wk_ref[at, :], wv_ref[at, :]
        ctx = nt(dkc_ref[...], wk) + nt(dvc_ref[...], wv)
        (csend_ref if p % 2 else ckeep_ref)[p // 2] = ctx.astype(BF16)
    for p in range(count):
        at = pl.ds(pl.multiple_of((idx ^ p) * width, width), width)
        own = nt(dq_ref[...], wq_ref[at, :]) + nt(dk_ref[...], wk_ref[at, :]) + nt(dv_ref[...], wv_ref[at, :])
        (nsend_ref if p % 2 else nkeep_ref)[p // 2] = own.astype(BF16)


def feed_kernel(parts, tile, seq, info_ref, x_ref, grad_ref, gain_ref, up_ref, down_ref, *rest):
    att_refs, wo_refs = rest[:parts], rest[parts : 2 * parts]
    mid_ref, n2_ref, act_ref, pre_ref, cot_ref, keep_ref, send_ref, okeep_ref, osend_ref = rest[2 * parts :]
    model = x_ref.shape[1]
    half = model // 2
    mine, limit = info_ref[1], info_ref[2 + seq]
    mid = x_ref[...].astype(F32)
    got = nn(att_refs[0][...], wo_refs[0][...])
    for p in range(1, parts):
        got = got + nn(att_refs[p][...], wo_refs[p][...])
    mid = mid + got
    mid_ref[...] = mid
    inv = lax.rsqrt(jnp.sum(mid * mid, -1, keepdims=True) * (1.0 / model) + EPS)
    n2_ref[...] = (mid * inv * gain_ref[...]).astype(BF16)
    place = lax.broadcasted_iota(jnp.int32, (tile, 1), 0) + pl.program_id(0) * tile
    cot = jnp.where(place < limit, grad_ref[...].astype(F32), 0.0).astype(BF16)
    cot_ref[...] = cot
    pre = nn(n2_ref[...], up_ref[...])
    cdf = 0.5 * (1.0 + lax.erf(pre * 0.7071067811865476))
    pdf = jnp.exp(pre * pre * -0.5) * 0.3989422804014327
    act_ref[...] = (pre * cdf).astype(BF16)
    pull = nt(cot, down_ref[...])
    pre_ref[...] = (pull * (cdf + pre * pdf)).astype(BF16)
    near = pl.ds(pl.multiple_of(mine * half, half), half)
    far = pl.ds(pl.multiple_of((1 - mine) * half, half), half)
    send_ref[...] = nt(pre_ref[...], up_ref[far, :]).astype(BF16)
    keep_ref[...] = nt(pre_ref[...], up_ref[near, :]).astype(BF16)
    osend_ref[...] = nn(act_ref[...], down_ref[:, far]).astype(BF16)
    okeep_ref[...] = nn(act_ref[...], down_ref[:, near]).astype(BF16)


def outer_kernel(pairs, *refs):
    out_ref = refs[-1]
    total = tn(refs[0][...], refs[1][...])
    for p in range(1, pairs):
        total = total + tn(refs[2 * p][...], refs[2 * p + 1][...])
    out_ref[...] = total.astype(BF16)


def outer(lefts, rights, tile):
    rows = lefts[0].shape[1]
    cols = rights[0].shape[1]
    tile = min(tile, rows)
    args, specs = [], []
    flops = 0
    for a, b in zip(lefts, rights):
        args += [a, b]
        specs += [
            pl.BlockSpec((a.shape[0], tile), lambda i: (0, i)),
            pl.BlockSpec(b.shape, lambda i: (0, 0)),
        ]
        flops += 2 * a.shape[0] * rows * cols
    return pl.pallas_call(
        functools.partial(outer_kernel, len(lefts)),
        grid=(rows // tile,),
        in_specs=specs,
        out_specs=pl.BlockSpec((tile, cols), lambda i: (i, 0)),
        out_shape=sds((rows, cols), BF16),
        compiler_params=params(24),
        cost_estimate=cost(flops, 2 * rows * cols + sum(a.size * 2 for a in args)),
    )(*args)


def project_grad_kernel(seqs, info_ref, *refs):
    lows = refs[:seqs]
    dqs, dks, dvs = refs[seqs : 2 * seqs], refs[2 * seqs : 3 * seqs], refs[3 * seqs : 4 * seqs]
    ctx_ref = refs[4 * seqs]
    dkcs, dvcs = refs[4 * seqs + 1 : 5 * seqs + 1], refs[5 * seqs + 1 : 6 * seqs + 1]
    gq_ref, gk_ref, gv_ref = refs[6 * seqs + 1 :]
    for out_ref, grads, sides in ((gq_ref, dqs, None), (gk_ref, dks, dkcs), (gv_ref, dvs, dvcs)):
        total = 0.0
        for s in range(seqs):
            total = total + tn(lows[s][...], grads[s][...])
            if sides is not None:
                total = total + tn(ctx_ref[0, s * CTX : (s + 1) * CTX, :], sides[s][...])
        out_ref[...] = total.astype(BF16)


def gather_parts(value, axis):
    parts = [value]
    for bit in reversed(low_bits(lax.axis_size(axis))):
        parts = parts + [None] * 0 + [swap(p, axis, bit) for p in parts]
    count = len(parts)
    order = [0]
    for bit in reversed(low_bits(count)):
        order = order + [k ^ bit for k in order]
    out = [None] * count
    for k, p in zip(order, parts):
        out[k] = p
    return out


def add_low(a, b):
    return (a.astype(F32) + b.astype(F32)).astype(BF16)


def scatter_parts(keep, send, axis):
    bits = low_bits(lax.axis_size(axis))
    got = swap(send, axis, 1)
    for bit in bits[1:]:
        now = add_low(keep, got)
        keep, send = now[0::2], now[1::2]
        got = swap(send, axis, bit)
    return keep[0], got[0]


def local(
    inputs, out_grad, lengths, norm_gain, query_weight, key_weight, value_weight, out_weight,
    mlp_gain, up_weight, down_weight, decay_rate, state_input, state_output, skip_gain,
):
    seqs, block, model = inputs.shape
    width = query_weight.shape[1]
    units = up_weight.shape[1]
    heads = width // HD
    stride = block // CTX
    scale = HD ** (-0.5)
    tensor_count = lax.axis_size("tensor")
    idx = lax.axis_index("tensor")
    place = lax.axis_index("seq")
    mine = idx & 1
    rows = seqs * block
    seg = rows // SUB
    half = model // 2
    seq_bits = low_bits(lax.axis_size("seq"))
    info = jnp.concatenate([jnp.stack([idx, mine]).astype(jnp.int32), (lengths - place * block).astype(jnp.int32)])

    flat_in = inputs.reshape(rows, model)
    chan_start = idx * width
    in_chan = lax.dynamic_slice_in_dim(flat_in, chan_start, width, 1)
    gain_chan = lax.dynamic_slice_in_dim(norm_gain, chan_start, width, 0)
    root = jnp.sqrt(-jnp.expm1(-2.0 * decay_rate))
    coeff = root * state_input
    skip_row = skip_gain.reshape(1, width)
    gain_row = gain_chan.reshape(1, width)
    tiles = width // HD
    tab = pltpu.VMEM((NS, SUB, width), F32)

    wo_parts = gather_parts(out_weight, "tensor")

    normed_low, hat, inverse, seg_end, final = pl.pallas_call(
        functools.partial(enter_kernel, seqs, stride),
        in_specs=[vmem()] * 4,
        out_specs=[vmem()] * 5,
        out_shape=[
            sds((rows, model), BF16),
            sds((tiles, rows, HD), F32),
            sds((rows, 1), F32),
            sds((NS, SUB, width), F32),
            sds((seqs, NS, width), F32),
        ],
        scratch_shapes=[tab, tab],
        compiler_params=params(16),
        cost_estimate=cost(rows * model * 8, rows * model * 5),
        name="enter",
    )(flat_in, in_chan, norm_gain.reshape(1, model), decay_rate)

    def hop(blocks):
        return jnp.exp(-decay_rate * (jnp.asarray(blocks, F32) * block))[None]

    carry_in = carried(final, hop, "seq", True)

    tile = 256
    query, key_self, value_self = pl.pallas_call(
        qkv_kernel,
        grid=(rows // tile,),
        in_specs=[pl.BlockSpec((tile, model), lambda i: (i, 0))]
        + [pl.BlockSpec((model, width), lambda i: (0, 0))] * 3,
        out_specs=[pl.BlockSpec((tile, width), lambda i: (i, 0))] * 3,
        out_shape=[sds((rows, width), BF16)] * 3,
        compiler_params=params(16),
        cost_estimate=cost(6 * rows * model * width, rows * model * 2 + 3 * model * width * 2),
        name="qkv",
    )(normed_low, query_weight, key_weight, value_weight)

    ctx_low, entry = pl.pallas_call(
        functools.partial(context_kernel, seqs, stride),
        in_specs=[vmem()] * 8,
        out_specs=[vmem()] * 2,
        out_shape=[sds((seqs * CTX, width), BF16), sds((NS, SUB, width), F32)],
        scratch_shapes=[tab, tab, tab, pltpu.VMEM((tiles, seqs * CTX, HD), F32)],
        compiler_params=params(16),
        cost_estimate=cost(rows * width * NS * 4, rows * width * 4),
        name="context",
    )(hat, seg_end, carry_in, decay_rate, coeff, state_output, skip_row, gain_row)
    ctx_parts = gather_parts(ctx_low, "tensor")

    def rows_of(s):
        return pl.BlockSpec((block, width), lambda i, s=s: (s, 0))

    def whole(shape):
        return pl.BlockSpec(shape, lambda i: (0,) * len(shape))

    attended, key_ctx, value_ctx, log_sum = [], [], [], []
    for s in range(seqs):
        a, kc, vc, ls = pl.pallas_call(
            functools.partial(attend_kernel, tensor_count, scale),
            grid=(1,),
            in_specs=[smem()]
            + [rows_of(s)] * 3
            + [whole((model, width))] * 2
            + [pl.BlockSpec((CTX, width), lambda i, s=s: (s, 0))] * tensor_count,
            out_specs=[whole((block, width)), whole((CTX, width)), whole((CTX, width)), whole((block, heads))],
            out_shape=[sds((block, width), BF16), sds((CTX, width), BF16), sds((CTX, width), BF16), sds((block, heads), F32)],
            compiler_params=params(24),
            cost_estimate=cost(4 * block * (block + CTX) * width + 4 * CTX * model * width, 4 * model * width + 8 * block * width, block * (block + CTX) * heads),
            name="attend",
        )(info, query, key_self, value_self, key_weight, value_weight, *ctx_parts)
        attended.append(a)
        key_ctx.append(kc)
        value_ctx.append(vc)
        log_sum.append(ls)

    flat_grad = out_grad.reshape(rows, model)
    gain2 = mlp_gain.reshape(1, model)
    att_parts = [gather_parts(a, "tensor") for a in attended]
    tile = 256
    steps = block // tile
    middle, normed2, act, pre_grad, cot, n2_near, n2_far, out_keep, out_send = ([] for _ in range(9))
    for s in range(seqs):

        def at(cols, s=s):
            return pl.BlockSpec((tile, cols), lambda i, s=s: (s * steps + i, 0))

        def own(cols):
            return pl.BlockSpec((tile, cols), lambda i: (i, 0))

        got = pl.pallas_call(
            functools.partial(feed_kernel, tensor_count, tile, s),
            grid=(steps,),
            in_specs=[smem(), at(model), at(model), whole((1, model)), whole((model, units)), whole((units, model))]
            + [own(width)] * tensor_count
            + [whole((width, model))] * tensor_count,
            out_specs=[own(model), own(model), own(units), own(units), own(model)] + [own(half)] * 4,
            out_shape=[sds((block, model), F32), sds((block, model), BF16), sds((block, units), BF16), sds((block, units), BF16), sds((block, model), BF16)]
            + [sds((block, half), BF16)] * 4,
            compiler_params=params(48),
            cost_estimate=cost(2 * block * model * (model + 4 * units), 3 * 2 * model * units + block * model * 16, block * units * 2),
            name="feed",
        )(info, flat_in, flat_grad, gain2, up_weight, down_weight, *att_parts[s], *wo_parts)
        middle.append(got[0])
        normed2.append(got[1])
        act.append(got[2])
        pre_grad.append(got[3])
        cot.append(got[4])
        near = add_low(got[5], swap(got[6], "tensor", 1))
        for bit in low_bits(tensor_count)[1:]:
            near = add_low(near, swap(near, "tensor", bit))
        n2_near.append(near)
        n2_far.append(swap(near, "tensor", 1))
        out_keep.append(got[7])
        out_send.append(got[8])

    down_grad = outer(act, cot, 256)
    up_grad = outer(normed2, pre_grad, 256)

    outputs = []
    for s in range(seqs):
        near = add_low(out_keep[s], swap(out_send[s], "tensor", 1))
        for bit in low_bits(tensor_count)[1:]:
            near = add_low(near, swap(near, "tensor", bit))
        mid_near = lax.dynamic_slice_in_dim(middle[s], mine * half, half, 1)
        near = (mid_near + near.astype(F32)).astype(BF16)
        far = swap(near, "tensor", 1)
        outputs.append(jnp.where(mine == 0, jnp.concatenate([near, far], 1), jnp.concatenate([far, near], 1)))
    outputs = jnp.stack(outputs)

    pairs = tensor_count // 2
    mid_low, mid_slice, gain2_part, dq, dk, dv, dkc, dvc, c_keep, c_send, n_keep, n_send = ([] for _ in range(12))
    for s in range(seqs):
        got = pl.pallas_call(
            functools.partial(attend_back_kernel, s, scale),
            grid=(1,),
            in_specs=[smem(), whole((block, model)), whole((block, half)), whole((block, half)), pl.BlockSpec((block, model), lambda i, s=s: (s, 0)), whole((1, model)), whole((width, model))]
            + [rows_of(s)] * 3
            + [whole((CTX, width))] * 2
            + [whole((block, heads))]
            + [whole((model, width))] * 3,
            out_specs=[whole((block, model)), whole((block, width)), whole((1, model))]
            + [whole((block, width))] * 3
            + [whole((CTX, width))] * 2
            + [whole((pairs, CTX, width))] * 2
            + [whole((pairs, block, width))] * 2,
            out_shape=[sds((block, model), BF16), sds((block, width), F32), sds((1, model), F32)]
            + [sds((block, width), BF16)] * 3
            + [sds((CTX, width), BF16)] * 2
            + [sds((pairs, CTX, width), BF16)] * 2
            + [sds((pairs, block, width), BF16)] * 2,
            scratch_shapes=[pltpu.VMEM((block, model), BF16), pltpu.VMEM((block, model), F32)]
            + [pltpu.VMEM((block, HD), F32)] * 2
            + [pltpu.VMEM((CTX, HD), F32)] * 2,
            compiler_params=params(32),
            cost_estimate=cost(10 * block * (block + CTX) * width + 8 * block * model * width, block * model * 12 + 8 * model * width, block * (block + CTX) * heads),
            name="attend_back",
        )(info, middle[s], n2_near[s], n2_far[s], flat_grad, gain2, out_weight, query, key_self, value_self, key_ctx[s], value_ctx[s], log_sum[s], query_weight, key_weight, value_weight)
        for slot, value in zip((mid_low, mid_slice, gain2_part, dq, dk, dv, dkc, dvc, c_keep, c_send, n_keep, n_send), got):
            slot.append(value)

    ctx_near, ctx_far = scatter_parts(jnp.concatenate(c_keep, 1), jnp.concatenate(c_send, 1), "tensor")
    n1_share = []
    for s in range(seqs):
        near, far = scatter_parts(n_keep[s], n_send[s], "tensor")
        n1_share.append(near.astype(F32) + far.astype(F32))

    ctx_grad, segb_end, lead = pl.pallas_call(
        functools.partial(lead_kernel, seqs, stride),
        in_specs=[vmem()] * 3,
        out_specs=[vmem()] * 3,
        out_shape=[sds((tiles, seqs * CTX, HD), F32), sds((NS, SUB, width), F32), sds((seqs, NS, width), F32)],
        scratch_shapes=[tab],
        compiler_params=params(16),
        cost_estimate=cost(seqs * CTX * width * NS * 2, seqs * CTX * width * 4),
        name="lead",
    )(ctx_near, ctx_far, decay_rate)
    carry_back = carried(lead, hop, "seq", False)

    out_weight_grad = outer(attended, mid_low, 256)
    ctx_stack = jnp.stack(ctx_parts)
    query_weight_grad, key_weight_grad, value_weight_grad = pl.pallas_call(
        functools.partial(project_grad_kernel, seqs),
        grid_spec=pltpu.PrefetchScalarGridSpec(
            num_scalar_prefetch=1,
            grid=(tensor_count,),
            in_specs=[pl.BlockSpec((block, width), lambda i, info, s=s: (s, i)) for s in range(seqs)]
            + [pl.BlockSpec((block, width), lambda i, info: (0, 0))] * (3 * seqs)
            + [pl.BlockSpec((1, seqs * CTX, width), lambda i, info: (i ^ info[0], 0, 0))]
            + [pl.BlockSpec((CTX, width), lambda i, info: (0, 0))] * (2 * seqs),
            out_specs=[pl.BlockSpec((width, width), lambda i, info: (i, 0))] * 3,
        ),
        out_shape=[sds((model, width), BF16)] * 3,
        compiler_params=params(24),
        cost_estimate=cost(6 * rows * model * width, rows * model * 2 + 6 * rows * width),
        name="project_grad",
    )(info, *([normed_low] * seqs), *dq, *dk, *dv, ctx_stack, *dkc, *dvc)

    chan_grad, rate_grad, sin_grad, sout_grad, skip_grad = pl.pallas_call(
        functools.partial(state_back_kernel, seqs, stride),
        in_specs=[vmem()] * 11,
        out_specs=[vmem()] * 5,
        out_shape=[sds((tiles, rows, HD), F32)] + [sds((NS, width), F32)] * 3 + [sds((1, width), F32)],
        scratch_shapes=[tab, tab, pltpu.VMEM((stride, NS, SUB, width), F32), tab, pltpu.VMEM((seg // stride + 1, NS, SUB, width), F32), pltpu.VMEM((stride + 2, NS, width), F32)],
        compiler_params=params(24),
        cost_estimate=cost(rows * width * NS * 12, rows * width * 12),
        name="state_back",
    )(hat, ctx_grad, entry, segb_end, carry_back, decay_rate, root, state_input, state_output, skip_row, gain_row)

    n1_grad = jnp.concatenate(n1_share, 0) + jnp.concatenate([chan_grad[t] for t in range(tiles)], 1)
    hat_chan = in_chan.astype(F32) * inverse
    norm_gain_grad = jnp.sum(n1_grad * hat_chan, 0)
    h1 = n1_grad * gain_chan
    total = jnp.sum(h1 * hat_chan, -1).reshape(rows // 128, 128)
    for bit in low_bits(tensor_count):
        total = total + swap(total, "tensor", bit)
    mid_chan = jnp.concatenate(mid_slice, 0)
    input_grad = mid_chan + inverse * (h1 - hat_chan * (total.reshape(rows, 1) / model))
    input_grad = input_grad.astype(BF16).reshape(seqs, block, width)

    mlp_gain_grad = sum(gain2_part)
    small = jnp.concatenate([rate_grad, sin_grad, sout_grad, skip_grad, norm_gain_grad.reshape(1, width), mlp_gain_grad.reshape(model // width, width)], 0)
    for bit in seq_bits:
        small = small + swap(small, "seq", bit)

    big = lax.psum((down_grad, up_grad), "seq")
    rest = lax.psum((query_weight_grad, key_weight_grad, value_weight_grad, out_weight_grad), "seq")
    return (
        outputs,
        input_grad,
        small[3 * NS + 1],
        rest[0].astype(F32),
        rest[1].astype(F32),
        rest[2].astype(F32),
        rest[3].astype(F32),
        small[3 * NS + 2 :].reshape(model),
        big[1].astype(F32),
        big[0].astype(F32),
        small[:NS],
        small[NS : 2 * NS],
        small[2 * NS : 3 * NS],
        small[3 * NS],
    )


def solution(mesh):
    in_specs = (
        P(None, "seq", None),
        P(None, "seq", None),
        P(),
        P(),
        P(None, "tensor"),
        P(None, "tensor"),
        P(None, "tensor"),
        P("tensor", None),
        P(),
        P(None, "tensor"),
        P("tensor", None),
        P(None, "tensor"),
        P(None, "tensor"),
        P(None, "tensor"),
        P("tensor"),
    )
    out_specs = (
        P(None, "seq", None),
        P(None, "seq", "tensor"),
        P("tensor"),
        P(None, "tensor"),
        P(None, "tensor"),
        P(None, "tensor"),
        P("tensor", None),
        P(),
        P(None, "tensor"),
        P("tensor", None),
        P(None, "tensor"),
        P(None, "tensor"),
        P(None, "tensor"),
        P("tensor"),
    )
    return jax.shard_map(local, mesh=mesh, in_specs=in_specs, out_specs=out_specs, check_vma=False)
```

time: 1340 us -> 386 us (0.29)
  matrix products: 521 us -> 0 us
  local copies, waits for them, and re-layouts: 314 us -> 21.4 us
  blocking collectives: 177 us -> 0 us
  other arithmetic: 205 us -> 30.2 us
  waiting for transfers between devices: 103 us -> 207 us
  Pallas kernels: 0 us -> 80.5 us
  starting transfers between devices: 0.68 us -> 31 us
    dot_general x42 -> x0, matrix products: 521 us -> none  [the longest x4 451 us: run_states(): jnp.einsum('tsnc,gsnc->gtnc', power_table(rate, inner_lag), pieces, preci...]
    all_gather x5 -> x0, blocking collectives: 134 us -> none  [the longest x2 63.5 us: carried_in(): lax.all_gather(a.astype(kind), axis)]
    add x16 -> x7, other arithmetic: 102 us -> 0.15 us  [the longest x2 0.11 us: local(): n1_share.append(near.astype(F32) + far.astype(F32))]
    ppermute x0 -> x41, waiting for transfers between devices: none -> 92.4 us  [swap(): return lax.ppermute(value, axis, [(i, i ^ bit) for i in range(count)])]
    pallas_call x0 -> x15, Pallas kernels: none -> 80.5 us  [the longest x2 21.1 us: local(): pl.pallas_call(functools.partial(feed_kernel, tensor_count, tile, s), gri...]
    while x69 -> x0, local copies, waits for them, and re-layouts: 75.3 us -> none
    add x4 -> x0, local copies, waits for them, and re-layouts: 73.1 us -> none  [run_states(): full = inner + reach_pow[None] * entering[:, None]]
    slice x14 -> x5, local copies, waits for them, and re-layouts: 66.7 us -> 1.9 us  [the longest x3 0.71 us: scatter_parts(): keep, send = (now[0::2], now[1::2])]
  transfers between devices with their start and end apart: 7 -> 42, of which waited for: 2 -> 20; matrix products, arithmetic and copies ran while one was open for 36% -> 6% of each run, Pallas kernels for 0% -> 20%
where the time goes in v1:
time: 386 us; the launch traced here: 385 us
  waiting for transfers between devices  207 us (54%)
  Pallas kernels  80.5 us (21%)
  starting transfers between devices  31 us (8%)
  other arithmetic  30.2 us (8%)
  local copies, waits for them, and re-layouts  21.4 us (6%)
  between operations  15.2 us (4%)
    psum x1, waiting for transfers between devices, local(): lax.psum((query_weight_grad, key_weight_grad, value_weight_grad, out_weig...  114 us
    ppermute x41, waiting for transfers between devices, swap(): return lax.ppermute(value, axis, [(i, i ^ bit) for i in range(count)])  92.4 us
    ppermute x41, starting transfers between devices, swap(): return lax.ppermute(value, axis, [(i, i ^ bit) for i in range(count)])  31 us
    pallas_call x2, Pallas kernels, local(): pl.pallas_call(functools.partial(feed_kernel, tensor_count, tile, s), gri...  21.1 us
    unnamed x190, local copies, waits for them, and re-layouts  17.5 us
    pallas_call x1, Pallas kernels, local(): pl.pallas_call(functools.partial(state_back_kernel, seqs, stride), in_spe...  15.4 us
    pallas_call x2, Pallas kernels, local(): pl.pallas_call(functools.partial(attend_back_kernel, s, scale), grid=(1,)...  13.7 us
    pallas_call x3, Pallas kernels, outer(): pl.pallas_call(functools.partial(outer_kernel, len(lefts)), grid=(rows //...  9.66 us
  transfers between devices with their start and end apart: 42, of which 20 were waited for; matrix products, arithmetic and copies ran while one was open for 6% of the time, Pallas kernels for 20%

profile of v1, /device:TPU:0, one launch (start us, length us, event | category | flops | bytes accessed | tf_op | source)
XLA Modules:
  0.0 385.1 jit_solution(15853418445092870201)
XLA Ops:
  7.3 1.1 constant_dynamic-slice_fusion.xc_ref
  8.4 1.6 copy-done.12
  11.4 4.1 %enter.1 = (bf16[1024,1024]{1,0:T(8,128)(2,1)S(1)}, f32[2,1024,128]{2,1,0:T(8,128)S(1)}, f32[1024,1]{1,0:T(8,128)S(1)}, f32[16,8,256]{2,1,0:T(8,128)S(1)}, f32[2,16,256]{2,1,0:T(8,128)S(1)}) custom-call(bf16[1024,1024]{1,0:T(8,128)(2,1)S(1)} %bitcast.47, bf16[1024,256]{1,0:T(8,128)(2,1)S(1)} %constant_dynamic-slice_fusion.xc_ref, f32[1,1024]{1,0:T(1,128)S(1)} %bitcast.60, ...), custom_call_target="tpu_custom_call" | custom-call | flops 8388608 | bytes 5242880 | tf_op jit(solution)/shard_map/enter/pallas_call | solution.py:583
  17.3 2.9 collective-permute-start
  20.9 1.2 collective-permute-done
  22.1 2.2 collective-permute-start.1
  24.3 1.9 collective-permute-done.1
  26.8 3.0 collective-permute-start.2
  29.8 1.5 collective-permute-start.10
  32.2 1.2 copy-done.19
  33.4 2.4 context.1
  36.5 1.7 collective-permute-start.4
  38.7 5.3 %collective-permute-done.4.rest_2_ = bf16[256,256]{1,0:T(8,128)(2,1)S(1)} collective-permute-done((bf16[256,256]{1,0:T(8,128)(2,1)S(1)}, bf16[256,256]{1,0:T(8,128)(2,1)S(1)}, u32[]{:S(2)}, u32[]{:S(2)}) %collective-permute-start.4) | collective-permute-done | bytes 131104 | tf_op jit(solution)/shard_map/ppermute | solution.py:34
  44.0 1.0 copy-done.21
  45.0 2.3 qkv.1
  50.5 1.0 copy-done.3
  51.5 1.0 copy-done.6
  52.6 1.0 copy-done.9
  53.6 3.1 attend.3
  56.7 1.6 collective-permute-start.16
  58.5 3.1 attend.2
  62.2 3.7 collective-permute-done.16.rest_2_
  66.4 4.7 %collective-permute-done.7.rest_2_ = bf16[512,256]{1,0:T(8,128)(2,1)S(1)} collective-permute-done((bf16[512,256]{1,0:T(8,128)(2,1)S(1)}, bf16[512,256]{1,0:T(8,128)(2,1)S(1)}, u32[]{:S(2)}, u32[]{:S(2)}) %collective-permute-start.7) | collective-permute-done | bytes 262176 | tf_op jit(solution)/shard_map/ppermute | solution.py:34
  71.1 10.6 %feed.3 = (f32[512,1024]{1,0:T(8,128)}, bf16[512,1024]{1,0:T(8,128)(2,1)}, bf16[512,1024]{1,0:T(8,128)(2,1)}, bf16[512,1024]{1,0:T(8,128)(2,1)}, bf16[512,1024]{...) custom-call(s32[4]{0:T(128)S(1)} %pad_add_fusion.idx_ref.info_ref, ...), custom_call_target="tpu_custom_call" | custom-call | flops 5368709120 | bytes 14680064 | tf_op jit(solution)/shard_map/feed/pallas_call | solution.py:670
  83.1 10.5 %feed.2 = (f32[512,1024]{1,0:T(8,128)}, bf16[512,1024]{1,0:T(8,128)(2,1)}, bf16[512,1024]{1,0:T(8,128)(2,1)}, bf16[512,1024]{1,0:T(8,128)(2,1)}, bf16[512,1024]{...) custom-call(s32[4]{0:T(128)S(1)} %pad_add_fusion.idx_ref.info_ref, ...), custom_call_target="tpu_custom_call" | custom-call | flops 5368709120 | bytes 14680064 | tf_op jit(solution)/shard_map/feed/pallas_call | solution.py:670
  93.8 1.6 collective-permute-start.25
  95.7 1.6 collective-permute-start.22
  97.3 1.1 pad_maximum_fusion.1.refs_8_
  98.5 10.1 %collective-permute-done.25 = bf16[512,512]{1,0:T(8,128)(2,1)S(1)} collective-permute-done((bf16[512,512]{1,0:T(8,128)(2,1)S(1)}, bf16[512,512]{1,0:T(8,128)(2,1)S(1)}, u32[]{:S(2)}, u32[]{:S(2)}) %collective-permute-start.25) | collective-permute-done | bytes 524320 | tf_op jit(solution)/shard_map/ppermute | solution.py:34
  108.8 10.6 %collective-permute-done.22 = bf16[512,512]{1,0:T(8,128)(2,1)S(1)} collective-permute-done((bf16[512,512]{1,0:T(8,128)(2,1)S(1)}, bf16[512,512]{1,0:T(8,128)(2,1)S(1)}, u32[]{:S(2)}, u32[]{:S(2)}) %collective-permute-start.22) | collective-permute-done | bytes 524320 | tf_op jit(solution)/shard_map/ppermute | solution.py:34
  119.7 4.1 %shard_map.256 = bf16[1024,1024]{1,0:T(8,128)(2,1)} custom-call(bf16[512,1024]{1,0:T(8,128)(2,1)S(1)} %copy-done.75, bf16[512,1024]{1,0:T(8,128)(2,1)S(1)} %copy-done.76, bf16[512,1024]{1,0:T(8,128)(2,1)S(1)} %copy-done.71, bf16[512,1024]{1,0:T(8,128)(2,1)S(1)} %copy-done.72), custom_call_target="tpu_custom_call" | custom-call | flops 2147483648 | bytes 6291456 | tf_op jit(solution)/shard_map/pallas_call | solution.py:496
  123.9 4.1 %shard_map.255 = bf16[1024,1024]{1,0:T(8,128)(2,1)} custom-call(bf16[512,1024]{1,0:T(8,128)(2,1)S(1)} %copy-done.73, bf16[512,1024]{1,0:T(8,128)(2,1)S(1)} %copy-done.74, bf16[512,1024]{1,0:T(8,128)(2,1)S(1)} %copy-done.69, bf16[512,1024]{1,0:T(8,128)(2,1)S(1)} %copy-done.70), custom_call_target="tpu_custom_call" | custom-call | flops 2147483648 | bytes 6291456 | tf_op jit(solution)/shard_map/pallas_call | solution.py:496
  128.0 6.9 %attend_back.3 = (bf16[512,1024]{1,0:T(8,128)(2,1)S(1)}, f32[512,256]{1,0:T(8,128)S(1)}, f32[1,1024]{1,0:T(1,128)S(1)}, bf16[512,256]{1,0:T(8,128)(2,1)S(1)}, bf...) custom-call(s32[4]{0:T(128)S(1)} %pad_add_fusion.idx_ref.info_ref, ...), custom_call_target="tpu_custom_call" | custom-call | flops 1912602624 | bytes 8388608 | tf_op jit(solution)/shard_map/attend_back/pallas_call | solution.py:713
  136.5 6.9 %attend_back.2 = (bf16[512,1024]{1,0:T(8,128)(2,1)S(1)}, f32[512,256]{1,0:T(8,128)S(1)}, f32[1,1024]{1,0:T(1,128)S(1)}, bf16[512,256]{1,0:T(8,128)(2,1)S(1)}, bf...) custom-call(s32[4]{0:T(128)S(1)} %pad_add_fusion.idx_ref.info_ref, ...), custom_call_target="tpu_custom_call" | custom-call | flops 1912602624 | bytes 8388608 | tf_op jit(solution)/shard_map/attend_back/pallas_call | solution.py:713
  143.5 4.6 %project_grad.1 = (bf16[1024,256]{1,0:T(8,128)(2,1)}, bf16[1024,256]{1,0:T(8,128)(2,1)}, bf16[1024,256]{1,0:T(8,128)(2,1)}) custom-call(s32[4]{0:T(128)S(1)} %pad_add_fusion.idx_ref.info_ref, bf16[1024,1024]{1,0:T(8,128)(2,1)S(1)} %get-tuple-element.85.x_ref.refs_0_.refs_1_, bf16[1024,1024]{1,0:T(8,128)(2,1)S(1)} %get-tuple-element.85.x_ref.refs_0_.refs_1_, ...), custom_call_target="tpu_custom_call" | custom-call | flops 1610612736 | bytes 3670016 | tf_op jit(solution)/shard_map/project_grad/pallas_call | solution.py:761
  148.1 1.5 shard_map.254
  151.2 1.2 add_convert_fusion.8
  152.4 1.6 collective-permute-start.19
  156.4 1.5 collective-permute-start.32
  157.8 9.4 %collective-permute-done.19 = bf16[512,512]{1,0:T(8,128)(2,1)S(1)} collective-permute-done((bf16[512,512]{1,0:T(8,128)(2,1)S(1)}, bf16[512,512]{1,0:T(8,128)(2,1)S(1)}, u32[]{:S(2)}, u32[]{:S(2)}) %collective-permute-start.19) | collective-permute-done | bytes 524320 | tf_op jit(solution)/shard_map/ppermute | solution.py:34
  168.5 12.0 %collective-permute-done.32 = bf16[1,256,256]{2,1,0:T(8,128)(2,1)S(1)} collective-permute-done((bf16[1,256,256]{2,1,0:T(8,128)(2,1)}, bf16[1,256,256]{2,1,0:T(8,128)(2,1)S(1)}, u32[]{:S(2)}, u32[]{:S(2)}) %collective-permute-start.32) | collective-permute-done | bytes 131104 | tf_op jit(solution)/shard_map/ppermute | solution.py:34
  181.5 1.6 collective-permute-start.33
  183.1 1.4 add_convert_fusion.9
  185.5 1.9 collective-permute-start.34
  187.6 3.1 maximum_select_fusion.1
  190.7 1.5 collective-permute-done.34
  192.3 1.3 maximum_select_fusion
  193.6 6.1 %collective-permute-done.35 = f32[2,16,256]{2,1,0:T(8,128)S(1)} collective-permute-done((f32[2,16,256]{2,1,0:T(8,128)S(1)}, f32[2,16,256]{2,1,0:T(8,128)S(1)}, u32[]{:S(2)}, u32[]{:S(2)}) %collective-permute-start.35) | collective-permute-done | bytes 32800 | tf_op jit(solution)/shard_map/ppermute | solution.py:34
  199.7 15.4 %state_back.1 = (f32[2,1024,128]{2,1,0:T(8,128)S(1)}, f32[16,256]{1,0:T(8,128)S(1)}, f32[16,256]{1,0:T(8,128)S(1)}, f32[16,256]{1,0:T(8,128)S(1)}, f32[1,256]{1,0:T(1,128)S(1)}) custom-call(f32[2,1024,128]{2,1,0:T(8,128)S(1)} %copy-done.20, f32[2,256,128]{2,1,0:T(8,128)S(1)} %get-tuple-element.122.grad_ref, f32[16,8,256]{2,1,0:T(8,128)S(1)} %copy-done.41, ...), custom_call_target="tpu_custom_call" | custom-call | flops 50331648 | bytes 3145728 | tf_op jit(solution)/shard_map/state_back/pallas_call | solution.py:778
  215.4 1.7 collective-permute-start.30
  217.8 6.9 %collective-permute-done.30 = bf16[1,512,256]{2,1,0:T(8,128)(2,1)S(1)} collective-permute-done((bf16[1,512,256]{2,1,0:T(8,128)(2,1)S(1)}, bf16[1,512,256]{2,1,0:T(8,128)(2,1)S(1)}, u32[]{:S(2)}, u32[]{:S(2)}) %collective-permute-start.30) | collective-permute-done | bytes 262176 | tf_op jit(solution)/shard_map/ppermute | solution.py:34
  224.7 3.6 collective-permute-done.28
  230.3 1.8 collective-permute-start.37
  232.1 3.1 pad_maximum_fusion
  235.3 7.4 %collective-permute-done.39 = f32[54,256]{1,0:T(8,128)S(1)} collective-permute-done((f32[54,256]{1,0:T(8,128)S(1)}, f32[54,256]{1,0:T(8,128)S(1)}, u32[]{:S(2)}, u32[]{:S(2)}) %collective-permute-start.39) | collective-permute-done | bytes 55328 | tf_op jit(solution)/shard_map/ppermute | solution.py:34
  243.0 1.2 fusion
  244.2 6.4 %collective-permute-done.40 = f32[54,256]{1,0:T(8,128)S(1)} collective-permute-done((f32[54,256]{1,0:T(8,128)S(1)}, f32[54,256]{1,0:T(8,128)S(1)}, u32[]{:S(2)}, u32[]{:S(2)}) %collective-permute-start.40) | collective-permute-done | bytes 55328 | tf_op jit(solution)/shard_map/ppermute | solution.py:34
  252.4 114.4 %all-reduce.3.cloned.1.call-done = (bf16[1024,256]{1,0:T(8,128)(2,1)}, bf16[1024,256]{1,0:T(8,128)(2,1)}, bf16[1024,256]{1,0:T(8,128)(2,1)}, bf16[256,1024]{1,0:...) async-done(((bf16[1024,256]{1,0:T(8,128)(2,1)}, bf16[1024,256]{1,0:T(8,128)(2,1)}, bf16[1024,256]{1,0:T(8,128)(2,1)}, bf16[256,1024]{1,0:T(8,128)(2,1)}, ...) | async-done | bytes 6291472 | tf_op jit(solution)/shard_map/psum | solution.py:806
  366.8 2.2 convert_element_type.210
  368.9 2.2 convert_element_type.211
  371.2 1.0 convert_element_type.212
  372.2 1.1 convert_element_type.213
  373.3 2.5 convert_element_type.214
  375.8 2.5 convert_element_type.215
  (278 shorter events, 27.3 us)
Async XLA Ops:
  7.2 13.0 %copy-start.39 = (f32[16,256]{1,0:T(8,128)S(1)}, f32[16,256]{1,0:T(8,128)}, u32[]{:S(2)}) copy-start(f32[16,256]{1,0:T(8,128)} %rate_ref.7) | copy-start | bytes 49156
  7.2 359.5 %all-reduce.3.cloned.1.call-start = ((), (), s32[]{:S(2)}) async-start(), calls=%async_computation | async-start | bytes 12582912 | tf_op jit(solution)/shard_map/psum | solution.py:806
  7.3 24.9 %copy-start.48 = (f32[16,256]{1,0:T(8,128)S(1)}, f32[16,256]{1,0:T(8,128)}, u32[]{:S(2)}) copy-start(f32[16,256]{1,0:T(8,128)} %sout_ref.3) | copy-start | bytes 49156
  7.3 24.9 %copy-start.57 = (f32[256]{0:T(256)S(1)}, f32[256]{0:T(256)}, u32[]{:S(2)}) copy-start(f32[256]{0:T(256)} %param.29) | copy-start | bytes 3076
  11.4 26.8 %copy-start.93 = (s32[2]{0:T(128)S(1)}, s32[2]{0:T(128)}, u32[]{:S(2)}) copy-start(s32[2]{0:T(128)} %param.17) | copy-start | bytes 28
  11.4 32.6 %copy-start = (bf16[1024,256]{1,0:T(8,128)(2,1)S(1)}, bf16[1024,256]{1,0:T(8,128)(2,1)}, u32[]{:S(2)}) copy-start(bf16[1024,256]{1,0:T(8,128)(2,1)} %wk_ref.9) | copy-start | bytes 1572868
  11.4 32.6 %copy-start.1 = (bf16[1024,256]{1,0:T(8,128)(2,1)S(1)}, bf16[1024,256]{1,0:T(8,128)(2,1)}, u32[]{:S(2)}) copy-start(bf16[1024,256]{1,0:T(8,128)(2,1)} %wv_ref.9) | copy-start | bytes 1572868
  17.3 4.8 %collective-permute-start = (f32[2,16,256]{2,1,0:T(8,128)S(1)}, f32[2,16,256]{2,1,0:T(8,128)S(1)}, u32[]{:S(2)}, u32[]{:S(2)}) collective-permute-start(f32[2,16,256]{2,1,0:T(8,128)S(1)} %get-tuple-element.91), channel_id=1, source_target_pairs={{0,4},{4,0},{8,12},{12,8},{16,20},{20,16},{24,28},{28,24},{1,5},{5... | collective-permute-start | bytes 98312 | tf_op jit(solution)/shard_map/ppermute | solution.py:34
  20.9 17.3 %copy-start.85 = (f32[16,256]{1,0:T(8,128)}, f32[16,256]{1,0:T(8,128)S(1)}, u32[]{:S(2)}) copy-start(f32[16,256]{1,0:T(8,128)S(1)} %get-tuple-element.178) | copy-start | bytes 49156
  20.9 17.3 %copy-start.87 = (f32[16,256]{1,0:T(8,128)}, f32[16,256]{1,0:T(8,128)S(1)}, u32[]{:S(2)}) copy-start(f32[16,256]{1,0:T(8,128)S(1)} %get-tuple-element.176) | copy-start | bytes 49156
  22.1 4.1 %collective-permute-start.1 = (f32[2,16,256]{2,1,0:T(8,128)S(1)}, f32[2,16,256]{2,1,0:T(8,128)S(1)}, u32[]{:S(2)}, u32[]{:S(2)}) collective-permute-start(f32[2,16,256]{2,1,0:T(8,128)S(1)} %add_select_fusion.7), channel_id=1, source_target_pairs={{0,8},{4,12},{8,0},{12,4},{16,24},{20,28},{24,16},{28,20},{1,9},{5... | collective-permute-start | bytes 98312 | tf_op jit(solution)/shard_map/ppermute | solution.py:34
  26.8 5.3 %collective-permute-start.2 = (f32[2,16,256]{2,1,0:T(8,128)}, f32[2,16,256]{2,1,0:T(8,128)S(1)}, u32[]{:S(2)}, u32[]{:S(2)}) collective-permute-start(f32[2,16,256]{2,1,0:T(8,128)} %add_select_fusion.6), channel_id=1, source_target_pairs={{0,16},{4,20},{8,24},{12,28},{16,0},{20,4},{24,8},{28,12},{1,17},{... | collective-permute-start | bytes 98312 | tf_op jit(solution)/shard_map/ppermute | solution.py:34
  29.8 28.5 %collective-permute-start.10 = (bf16[256,1024]{1,0:T(8,128)(2,1)}, bf16[256,1024]{1,0:T(8,128)(2,1)}, u32[]{:S(2)}, u32[]{:S(2)}) collective-permute-start(bf16[256,1024]{1,0:T(8,128)(2,1)} %wo_ref.3), channel_id=1, source_target_pairs={{0,2},{1,3},{2,0},{3,1},{4,6},{5,7},{6,4},{7,5},{8,10},{9,11},{10,... | collective-permute-start | bytes 1572872 | tf_op jit(solution)/shard_map/ppermute | solution.py:34
  31.4 34.5 %collective-permute-start.9 = (bf16[256,1024]{1,0:T(8,128)(2,1)}, bf16[256,1024]{1,0:T(8,128)(2,1)}, u32[]{:S(2)}, u32[]{:S(2)}) collective-permute-start(bf16[256,1024]{1,0:T(8,128)(2,1)} %wo_ref.3), channel_id=1, source_target_pairs={{0,1},{1,0},{2,3},{3,2},{4,5},{5,4},{6,7},{7,6},{8,9},{9,8},{10,11... | collective-permute-start | bytes 1572872 | tf_op jit(solution)/shard_map/ppermute | solution.py:34
  36.5 7.5 %collective-permute-start.4 = (bf16[256,256]{1,0:T(8,128)(2,1)S(1)}, bf16[256,256]{1,0:T(8,128)(2,1)S(1)}, u32[]{:S(2)}, u32[]{:S(2)}) collective-permute-start(bf16[256,256]{1,0:T(8,128)(2,1)S(1)} %get-tuple-element.92.rest_0_), channel_id=1, source_target_pairs={{0,2},{1,3},{2,0},{3,1},{4,6},{5,7},{6,4},{7,5},{8,10},{9,11},{10,... | collective-permute-start | bytes 393224 | tf_op jit(solution)/shard_map/ppermute | solution.py:34
  38.6 11.8 %collective-permute-start.3 = (bf16[256,256]{1,0:T(8,128)(2,1)S(1)}, bf16[256,256]{1,0:T(8,128)(2,1)S(1)}, u32[]{:S(2)}, u32[]{:S(2)}) collective-permute-start(bf16[256,256]{1,0:T(8,128)(2,1)S(1)} %get-tuple-element.92.rest_0_), channel_id=1, source_target_pairs={{0,1},{1,0},{2,3},{3,2},{4,5},{5,4},{6,7},{7,6},{8,9},{9,8},{10,11... | collective-permute-start | bytes 393224 | tf_op jit(solution)/shard_map/ppermute | solution.py:34
  43.9 6.5 %collective-permute-start.5 = (bf16[256,256]{1,0:T(8,128)(2,1)S(1)}, bf16[256,256]{1,0:T(8,128)(2,1)}, u32[]{:S(2)}, u32[]{:S(2)}) collective-permute-start(bf16[256,256]{1,0:T(8,128)(2,1)S(1)} %collective-permute-done.4.rest_2_), channel_id=1, source_target_pairs={{0,1},{1,0},{2,3},{3,2},{4,5},{5,4},{6,7},{7,6},{8,9},{9,8},{10,11... | collective-permute-start | bytes 393224 | tf_op jit(solution)/shard_map/ppermute | solution.py:34
  56.7 14.4 %copy-start.23 = (bf16[256,1024]{1,0:T(8,128)(2,1)S(1)}, bf16[256,1024]{1,0:T(8,128)(2,1)}, u32[]{:S(2)}) copy-start(bf16[256,1024]{1,0:T(8,128)(2,1)} %wo_ref.3) | copy-start | bytes 1572868
  56.7 14.4 %copy-start.55 = (f32[1024]{0:T(1024)S(1)}, f32[1024]{0:T(1024)}, u32[]{:S(2)}) copy-start(f32[1024]{0:T(1024)} %param.23) | copy-start | bytes 12292
  56.7 9.2 %collective-permute-start.16 = (bf16[512,256]{1,0:T(8,128)(2,1)S(1)}, bf16[512,256]{1,0:T(8,128)(2,1)S(1)}, u32[]{:S(2)}, u32[]{:S(2)}) collective-permute-start(bf16[512,256]{1,0:T(8,128)(2,1)S(1)} %get-tuple-element.97.rest_0_.refs_2_), channel_id=1, source_target_pairs={{0,2},{1,3},{2,0},{3,1},{4,6},{5,7},{6,4},{7,5},{8,10},{9,11},{10,... | collective-permute-start | bytes 786440 | tf_op jit(solution)/shard_map/ppermute | solution.py:34
  58.3 12.8 %collective-permute-start.11 = (bf16[256,1024]{1,0:T(8,128)(2,1)}, bf16[256,1024]{1,0:T(8,128)(2,1)S(1)}, u32[]{:S(2)}, u32[]{:S(2)}) collective-permute-start(bf16[256,1024]{1,0:T(8,128)(2,1)} %collective-permute-done.10.rest_6_), channel_id=1, source_target_pairs={{0,1},{1,0},{2,3},{3,2},{4,5},{5,4},{6,7},{7,6},{8,9},{9,8},{10,11... | collective-permute-start | bytes 1572872 | tf_op jit(solution)/shard_map/ppermute | solution.py:34
  61.6 9.5 %collective-permute-start.7 = (bf16[512,256]{1,0:T(8,128)(2,1)S(1)}, bf16[512,256]{1,0:T(8,128)(2,1)S(1)}, u32[]{:S(2)}, u32[]{:S(2)}) collective-permute-start(bf16[512,256]{1,0:T(8,128)(2,1)S(1)} %get-tuple-element.93.rest_0_.refs_0_), channel_id=1, source_target_pairs={{0,2},{1,3},{2,0},{3,1},{4,6},{5,7},{6,4},{7,5},{8,10},{9,11},{10,... | collective-permute-start | bytes 786440 | tf_op jit(solution)/shard_map/ppermute | solution.py:34
  62.2 8.9 %collective-permute-start.15 = (bf16[512,256]{1,0:T(8,128)(2,1)S(1)}, bf16[512,256]{1,0:T(8,128)(2,1)S(1)}, u32[]{:S(2)}, u32[]{:S(2)}) collective-permute-start(bf16[512,256]{1,0:T(8,128)(2,1)S(1)} %get-tuple-element.97.rest_0_.refs_2_), channel_id=1, source_target_pairs={{0,1},{1,0},{2,3},{3,2},{4,5},{5,4},{6,7},{7,6},{8,9},{9,8},{10,11... | collective-permute-start | bytes 786440 | tf_op jit(solution)/shard_map/ppermute | solution.py:34
  65.9 5.2 %collective-permute-start.17 = (bf16[512,256]{1,0:T(8,128)(2,1)S(1)}, bf16[512,256]{1,0:T(8,128)(2,1)S(1)}, u32[]{:S(2)}, u32[]{:S(2)}) collective-permute-start(bf16[512,256]{1,0:T(8,128)(2,1)S(1)} %collective-permute-done.16.rest_2_), channel_id=1, source_target_pairs={{0,1},{1,0},{2,3},{3,2},{4,5},{5,4},{6,7},{7,6},{8,9},{9,8},{10,11... | collective-permute-start | bytes 786440 | tf_op jit(solution)/shard_map/ppermute | solution.py:34
  65.9 17.2 %collective-permute-start.6 = (bf16[512,256]{1,0:T(8,128)(2,1)S(1)}, bf16[512,256]{1,0:T(8,128)(2,1)S(1)}, u32[]{:S(2)}, u32[]{:S(2)}) collective-permute-start(bf16[512,256]{1,0:T(8,128)(2,1)S(1)} %get-tuple-element.93.rest_0_.refs_0_), channel_id=1, source_target_pairs={{0,1},{1,0},{2,3},{3,2},{4,5},{5,4},{6,7},{7,6},{8,9},{9,8},{10,11... | collective-permute-start | bytes 786440 | tf_op jit(solution)/shard_map/ppermute | solution.py:34
  71.1 12.0 %collective-permute-start.8 = (bf16[512,256]{1,0:T(8,128)(2,1)S(1)}, bf16[512,256]{1,0:T(8,128)(2,1)S(1)}, u32[]{:S(2)}, u32[]{:S(2)}) collective-permute-start(bf16[512,256]{1,0:T(8,128)(2,1)S(1)} %collective-permute-done.7.rest_2_), channel_id=1, source_target_pairs={{0,1},{1,0},{2,3},{3,2},{4,5},{5,4},{6,7},{7,6},{8,9},{9,8},{10,11... | collective-permute-start | bytes 786440 | tf_op jit(solution)/shard_map/ppermute | solution.py:34
  82.5 11.2 %collective-permute-start.24 = (bf16[512,512]{1,0:T(8,128)(2,1)S(1)}, bf16[512,512]{1,0:T(8,128)(2,1)S(1)}, u32[]{:S(2)}, u32[]{:S(2)}) collective-permute-start(bf16[512,512]{1,0:T(8,128)(2,1)S(1)} %get-tuple-element.108), channel_id=1, source_target_pairs={{0,1},{1,0},{2,3},{3,2},{4,5},{5,4},{6,7},{7,6},{8,9},{9,8},{10,11... | collective-permute-start | bytes 1572872 | tf_op jit(solution)/shard_map/ppermute | solution.py:34
  93.6 2.0 collective-permute-start.21
  93.8 14.8 %collective-permute-start.25 = (bf16[512,512]{1,0:T(8,128)(2,1)S(1)}, bf16[512,512]{1,0:T(8,128)(2,1)S(1)}, u32[]{:S(2)}, u32[]{:S(2)}) collective-permute-start(bf16[512,512]{1,0:T(8,128)(2,1)S(1)} %add_convert_fusion.3), channel_id=1, source_target_pairs={{0,2},{1,3},{2,0},{3,1},{4,6},{5,7},{6,4},{7,5},{8,10},{9,11},{10,... | collective-permute-start | bytes 1572872 | tf_op jit(solution)/shard_map/ppermute | solution.py:34
  95.7 23.7 %collective-permute-start.22 = (bf16[512,512]{1,0:T(8,128)(2,1)S(1)}, bf16[512,512]{1,0:T(8,128)(2,1)S(1)}, u32[]{:S(2)}, u32[]{:S(2)}) collective-permute-start(bf16[512,512]{1,0:T(8,128)(2,1)S(1)} %add_convert_fusion.5), channel_id=1, source_target_pairs={{0,2},{1,3},{2,0},{3,1},{4,6},{5,7},{6,4},{7,5},{8,10},{9,11},{10,... | collective-permute-start | bytes 1572872 | tf_op jit(solution)/shard_map/ppermute | solution.py:34
  97.3 22.4 %copy-start.71 = (bf16[512,1024]{1,0:T(8,128)(2,1)S(1)}, bf16[512,1024]{1,0:T(8,128)(2,1)}, u32[]{:S(2)}) copy-start(bf16[512,1024]{1,0:T(8,128)(2,1)} %get-tuple-element.154.refs_2_) | copy-start | bytes 3145732
  97.3 22.4 %copy-start.72 = (bf16[512,1024]{1,0:T(8,128)(2,1)S(1)}, bf16[512,1024]{1,0:T(8,128)(2,1)}, u32[]{:S(2)}) copy-start(bf16[512,1024]{1,0:T(8,128)(2,1)} %get-tuple-element.155.refs_3_) | copy-start | bytes 3145732
  97.3 22.4 %copy-start.75 = (bf16[512,1024]{1,0:T(8,128)(2,1)S(1)}, bf16[512,1024]{1,0:T(8,128)(2,1)}, u32[]{:S(2)}) copy-start(bf16[512,1024]{1,0:T(8,128)(2,1)} %get-tuple-element.152.refs_0_) | copy-start | bytes 3145732
  97.3 22.4 %copy-start.76 = (bf16[512,1024]{1,0:T(8,128)(2,1)S(1)}, bf16[512,1024]{1,0:T(8,128)(2,1)}, u32[]{:S(2)}) copy-start(bf16[512,1024]{1,0:T(8,128)(2,1)} %get-tuple-element.153.refs_1_) | copy-start | bytes 3145732
  98.5 52.8 %collective-permute-start.18 = (bf16[512,512]{1,0:T(8,128)(2,1)}, bf16[512,512]{1,0:T(8,128)(2,1)}, u32[]{:S(2)}, u32[]{:S(2)}) collective-permute-start(bf16[512,512]{1,0:T(8,128)(2,1)} %get-tuple-element.100), channel_id=1, source_target_pairs={{0,1},{1,0},{2,3},{3,2},{4,5},{5,4},{6,7},{7,6},{8,9},{9,8},{10,11... | collective-permute-start | bytes 1572872 | tf_op jit(solution)/shard_map/ppermute | solution.py:34
  108.8 19.2 %collective-permute-start.26 = (bf16[512,512]{1,0:T(8,128)(2,1)S(1)}, bf16[512,512]{1,0:T(8,128)(2,1)S(1)}, u32[]{:S(2)}, u32[]{:S(2)}) collective-permute-start(bf16[512,512]{1,0:T(8,128)(2,1)S(1)} %add_convert_fusion.2.near_ref), channel_id=1, source_target_pairs={{0,1},{1,0},{2,3},{3,2},{4,5},{5,4},{6,7},{7,6},{8,9},{9,8},{10,11... | collective-permute-start | bytes 1572872 | tf_op jit(solution)/shard_map/ppermute | solution.py:34
  119.6 16.9 %collective-permute-start.23 = (bf16[512,512]{1,0:T(8,128)(2,1)S(1)}, bf16[512,512]{1,0:T(8,128)(2,1)S(1)}, u32[]{:S(2)}, u32[]{:S(2)}) collective-permute-start(bf16[512,512]{1,0:T(8,128)(2,1)S(1)} %add_convert_fusion.4.near_ref), channel_id=1, source_target_pairs={{0,1},{1,0},{2,3},{3,2},{4,5},{5,4},{6,7},{7,6},{8,9},{9,8},{10,11... | collective-permute-start | bytes 1572872 | tf_op jit(solution)/shard_map/ppermute | solution.py:34
  150.7 3.4 collective-permute-start.12
  152.4 14.8 %copy-start.17 = (f32[512,1024]{1,0:T(8,128)S(1)}, f32[512,1024]{1,0:T(8,128)}, u32[]{:S(2)}) copy-start(f32[512,1024]{1,0:T(8,128)} %get-tuple-element.98.mid_ref) | copy-start | bytes 6291460
  152.4 14.8 %collective-permute-start.19 = (bf16[512,512]{1,0:T(8,128)(2,1)S(1)}, bf16[512,512]{1,0:T(8,128)(2,1)S(1)}, u32[]{:S(2)}, u32[]{:S(2)}) collective-permute-start(bf16[512,512]{1,0:T(8,128)(2,1)S(1)} %add_convert_fusion.8), channel_id=1, source_target_pairs={{0,2},{1,3},{2,0},{3,1},{4,6},{5,7},{6,4},{7,5},{8,10},{9,11},{10,... | collective-permute-start | bytes 1572872 | tf_op jit(solution)/shard_map/ppermute | solution.py:34
  154.0 1.6 collective-permute-start.31
  155.0 13.2 %copy-start.37 = (f32[1024,1]{1,0:T(8,128)S(1)}, f32[1024,1]{1,0:T(8,128)}, u32[]{:S(2)}) copy-start(f32[1024,1]{1,0:T(8,128)} %copy-done.36) | copy-start | bytes 12292
  155.0 28.0 %collective-permute-start.13 = (bf16[512,512]{1,0:T(8,128)(2,1)}, bf16[512,512]{1,0:T(8,128)(2,1)}, u32[]{:S(2)}, u32[]{:S(2)}) collective-permute-start(bf16[512,512]{1,0:T(8,128)(2,1)} %add_convert_fusion.11), channel_id=1, source_target_pairs={{0,2},{1,3},{2,0},{3,1},{4,6},{5,7},{6,4},{7,5},{8,10},{9,11},{10,... | collective-permute-start | bytes 1572872 | tf_op jit(solution)/shard_map/ppermute | solution.py:34
  155.7 27.4 %copy-start.15 = (f32[512,1024]{1,0:T(8,128)S(1)}, f32[512,1024]{1,0:T(8,128)}, u32[]{:S(2)}) copy-start(f32[512,1024]{1,0:T(8,128)} %get-tuple-element.94.mid_ref) | copy-start | bytes 6291460
  156.4 24.1 %collective-permute-start.32 = (bf16[1,256,256]{2,1,0:T(8,128)(2,1)}, bf16[1,256,256]{2,1,0:T(8,128)(2,1)S(1)}, u32[]{:S(2)}, u32[]{:S(2)}) collective-permute-start(bf16[1,256,256]{2,1,0:T(8,128)(2,1)} %get-tuple-element.166), channel_id=1, source_target_pairs={{0,2},{1,3},{2,0},{3,1},{4,6},{5,7},{6,4},{7,5},{8,10},{9,11},{10,... | collective-permute-start | bytes 393224 | tf_op jit(solution)/shard_map/ppermute | solution.py:34
  168.2 16.3 %copy-start.64 = (bf16[2,512,256]{2,1,0:T(8,128)(2,1)S(1)}, bf16[2,512,256]{2,1,0:T(8,128)(2,1)}, u32[]{:S(2)}) copy-start(bf16[2,512,256]{2,1,0:T(8,128)(2,1)} %copy-done.63) | copy-start | bytes 1572868
  168.2 17.3 %copy-start.88 = (f32[16,256]{1,0:T(8,128)S(1)}, f32[16,256]{1,0:T(8,128)}, u32[]{:S(2)}) copy-start(f32[16,256]{1,0:T(8,128)} %copy-done.87) | copy-start | bytes 49156
  168.2 19.2 %collective-permute-start.20 = (bf16[512,512]{1,0:T(8,128)(2,1)}, bf16[512,512]{1,0:T(8,128)(2,1)}, u32[]{:S(2)}, u32[]{:S(2)}) collective-permute-start(bf16[512,512]{1,0:T(8,128)(2,1)} %add_convert_fusion.6), channel_id=1, source_target_pairs={{0,1},{1,0},{2,3},{3,2},{4,5},{5,4},{6,7},{7,6},{8,9},{9,8},{10,11... | collective-permute-start | bytes 1572872 | tf_op jit(solution)/shard_map/ppermute | solution.py:34
  168.5 16.6 %copy-start.66 = (bf16[2,512,256]{2,1,0:T(8,128)(2,1)S(1)}, bf16[2,512,256]{2,1,0:T(8,128)(2,1)}, u32[]{:S(2)}) copy-start(bf16[2,512,256]{2,1,0:T(8,128)(2,1)} %copy-done.65) | copy-start | bytes 1572868
  181.5 4.0 %collective-permute-start.33 = (f32[2,16,256]{2,1,0:T(8,128)S(1)}, f32[2,16,256]{2,1,0:T(8,128)S(1)}, u32[]{:S(2)}, u32[]{:S(2)}) collective-permute-start(f32[2,16,256]{2,1,0:T(8,128)S(1)} %get-tuple-element.125), channel_id=1, source_target_pairs={{0,4},{4,0},{8,12},{12,8},{16,20},{20,16},{24,28},{28,24},{1,5},{5... | collective-permute-start | bytes 98312 | tf_op jit(solution)/shard_map/ppermute | solution.py:34
  184.5 7.8 %collective-permute-start.14 = (bf16[512,512]{1,0:T(8,128)(2,1)S(1)}, bf16[512,512]{1,0:T(8,128)(2,1)S(1)}, u32[]{:S(2)}, u32[]{:S(2)}) collective-permute-start(bf16[512,512]{1,0:T(8,128)(2,1)S(1)} %add_convert_fusion.9), channel_id=1, source_target_pairs={{0,1},{1,0},{2,3},{3,2},{4,5},{5,4},{6,7},{7,6},{8,9},{9,8},{10,11... | collective-permute-start | bytes 1572872 | tf_op jit(solution)/shard_map/ppermute | solution.py:34
  184.6 30.6 %collective-permute-start.29 = (bf16[2,512,256]{2,1,0:T(8,128)(2,1)S(1)}, bf16[2,512,256]{2,1,0:T(8,128)(2,1)S(1)}, u32[]{:S(2)}, u32[]{:S(2)}) collective-permute-start(bf16[2,512,256]{2,1,0:T(8,128)(2,1)S(1)} %copy-done.64), channel_id=1, source_target_pairs={{0,1},{1,0},{2,3},{3,2},{4,5},{5,4},{6,7},{7,6},{8,9},{9,8},{10,11... | collective-permute-start | bytes 1572872 | tf_op jit(solution)/shard_map/ppermute | solution.py:34
  185.1 31.9 %collective-permute-start.27 = (bf16[2,512,256]{2,1,0:T(8,128)(2,1)S(1)}, bf16[2,512,256]{2,1,0:T(8,128)(2,1)S(1)}, u32[]{:S(2)}, u32[]{:S(2)}) collective-permute-start(bf16[2,512,256]{2,1,0:T(8,128)(2,1)S(1)} %copy-done.66), channel_id=1, source_target_pairs={{0,1},{1,0},{2,3},{3,2},{4,5},{5,4},{6,7},{7,6},{8,9},{9,8},{10,11... | collective-permute-start | bytes 1572872 | tf_op jit(solution)/shard_map/ppermute | solution.py:34
  185.5 6.7 %collective-permute-start.34 = (f32[2,16,256]{2,1,0:T(8,128)S(1)}, f32[2,16,256]{2,1,0:T(8,128)S(1)}, u32[]{:S(2)}, u32[]{:S(2)}) collective-permute-start(f32[2,16,256]{2,1,0:T(8,128)S(1)} %add_select_fusion.5), channel_id=1, source_target_pairs={{0,8},{4,12},{8,0},{12,4},{16,24},{20,28},{24,16},{28,20},{1,9},{5... | collective-permute-start | bytes 98312 | tf_op jit(solution)/shard_map/ppermute | solution.py:34
  190.7 24.5 %copy-start.29 = (bf16[2,512,256]{2,1,0:T(8,128)(2,1)S(1)}, bf16[2,512,256]{2,1,0:T(8,128)(2,1)}, u32[]{:S(2)}) copy-start(bf16[2,512,256]{2,1,0:T(8,128)(2,1)} %copy-done.28) | copy-start | bytes 1572868
  192.2 7.4 %collective-permute-start.35 = (f32[2,16,256]{2,1,0:T(8,128)S(1)}, f32[2,16,256]{2,1,0:T(8,128)S(1)}, u32[]{:S(2)}, u32[]{:S(2)}) collective-permute-start(f32[2,16,256]{2,1,0:T(8,128)S(1)} %add_select_fusion.4), channel_id=1, source_target_pairs={{0,16},{4,20},{8,24},{12,28},{16,0},{20,4},{24,8},{28,12},{1,17},{... | collective-permute-start | bytes 98312 | tf_op jit(solution)/shard_map/ppermute | solution.py:34
  193.6 23.4 %copy-start.31 = (bf16[2,512,256]{2,1,0:T(8,128)(2,1)S(1)}, bf16[2,512,256]{2,1,0:T(8,128)(2,1)}, u32[]{:S(2)}) copy-start(bf16[2,512,256]{2,1,0:T(8,128)(2,1)} %copy-done.30) | copy-start | bytes 1572868
  215.4 9.3 %collective-permute-start.30 = (bf16[1,512,256]{2,1,0:T(8,128)(2,1)S(1)}, bf16[1,512,256]{2,1,0:T(8,128)(2,1)S(1)}, u32[]{:S(2)}, u32[]{:S(2)}) collective-permute-start(bf16[1,512,256]{2,1,0:T(8,128)(2,1)S(1)} %slice.65), channel_id=1, source_target_pairs={{0,2},{1,3},{2,0},{3,1},{4,6},{5,7},{6,4},{7,5},{8,10},{9,11},{10,... | collective-permute-start | bytes 786440 | tf_op jit(solution)/shard_map/ppermute | solution.py:34
  217.2 11.2 %collective-permute-start.28 = (bf16[1,512,256]{2,1,0:T(8,128)(2,1)S(1)}, bf16[1,512,256]{2,1,0:T(8,128)(2,1)S(1)}, u32[]{:S(2)}, u32[]{:S(2)}) collective-permute-start(bf16[1,512,256]{2,1,0:T(8,128)(2,1)S(1)} %slice.63), channel_id=1, source_target_pairs={{0,2},{1,3},{2,0},{3,1},{4,6},{5,7},{6,4},{7,5},{8,10},{9,11},{10,... | collective-permute-start | bytes 786440 | tf_op jit(solution)/shard_map/ppermute | solution.py:34
  229.1 1.2 collective-permute-start.36
  229.2 6.0 %collective-permute-start.38 = (f32[54,256]{1,0:T(8,128)S(1)}, f32[54,256]{1,0:T(8,128)S(1)}, u32[]{:S(2)}, u32[]{:S(2)}) collective-permute-start(f32[54,256]{1,0:T(8,128)S(1)} %concatenate.83), channel_id=1, source_target_pairs={{0,4},{4,0},{8,12},{12,8},{16,20},{20,16},{24,28},{28,24},{1,5},{5... | collective-permute-start | bytes 165896 | tf_op jit(solution)/shard_map/ppermute | solution.py:34
  230.3 5.0 %collective-permute-start.37 = (f32[8,128]{1,0:T(8,128)S(1)}, f32[8,128]{1,0:T(8,128)S(1)}, u32[]{:S(2)}, u32[]{:S(2)}) collective-permute-start(f32[8,128]{1,0:T(8,128)S(1)} %bitcast_add_fusion), channel_id=1, source_target_pairs={{0,2},{1,3},{2,0},{3,1},{4,6},{5,7},{6,4},{7,5},{8,10},{9,11},{10,... | collective-permute-start | bytes 12296 | tf_op jit(solution)/shard_map/ppermute | solution.py:34
  235.2 7.5 %collective-permute-start.39 = (f32[54,256]{1,0:T(8,128)S(1)}, f32[54,256]{1,0:T(8,128)S(1)}, u32[]{:S(2)}, u32[]{:S(2)}) collective-permute-start(f32[54,256]{1,0:T(8,128)S(1)} %add.167), channel_id=1, source_target_pairs={{0,8},{4,12},{8,0},{12,4},{16,24},{20,28},{24,16},{28,20},{1,9},{5... | collective-permute-start | bytes 165896 | tf_op jit(solution)/shard_map/ppermute | solution.py:34
  242.7 7.9 %collective-permute-start.40 = (f32[54,256]{1,0:T(8,128)S(1)}, f32[54,256]{1,0:T(8,128)S(1)}, u32[]{:S(2)}, u32[]{:S(2)}) collective-permute-start(f32[54,256]{1,0:T(8,128)S(1)} %add.168), channel_id=1, source_target_pairs={{0,16},{4,20},{8,24},{12,28},{16,0},{20,4},{24,8},{28,12},{1,17},{... | collective-permute-start | bytes 165896 | tf_op jit(solution)/shard_map/ppermute | solution.py:34
  (72 other events, 417.7 us)
Sparse Core Ops, SparseCore 0:
  149.8 216.8 all-reduce.2
